TPU v7x, 256 devices: a whole 4x4x8 slice. The times are simulated.
256 devices in a mesh: seq: 32 (over x, y, core), tp: 8 (over z).
Axes of the slice: x: 4, y: 4, z: 8, core: 2. Of those that a mesh axis runs over, the one named last changes fastest.
Arguments:
- queries: bfloat16 [16384, 16, 128], P('seq', 'tp'), may hold values from -60 to 60
- keys: bfloat16 [16384, 8, 128], P('seq', 'tp'), may hold values from -60 to 60
- values: bfloat16 [16384, 8, 128], P('seq', 'tp'), may hold values from -5 to 5
- out_weight: bfloat16 [2048, 4608], P('tp'), may hold values from -0.125 to 0.125
- cotangent: bfloat16 [16384, 4608], P(('seq', 'tp')), may hold values from -5 to 5
- advantages: float32 [8], replicated, may hold values from -3 to 3
- lengths: int32 [8], replicated, may hold values from 1 to 6144, 16384 in all
Outputs:
- attention: bfloat16 [16384, 16, 128], P('seq', 'tp')
- d_queries: bfloat16 [16384, 16, 128], P('seq', 'tp')
- d_keys: bfloat16 [16384, 8, 128], P('seq', 'tp')
- d_values: bfloat16 [16384, 8, 128], P('seq', 'tp')
- d_wo_t: float32 [4608, 2048], P('seq', 'tp')
Inputs may be any that keep to these rules, and one draw needn't show every extreme that they name: `lengths`: the rollouts lie one after another along the tokens and together fill all 16384.
All inputs are finite; a program needn't handle non-finite values.
Results may differ from a plain program's by a relative error of at most 0.028.
Values may be sent and summed in bfloat16 or wider, within the bound.
A program may use at most 128 MiB of HBM per device.

v0:
```python
from functools import partial

import jax
import jax.numpy as jnp
from jax import lax
from jax.sharding import PartitionSpec as P

WINDOW = 4096


SCORE_SCALE = 1.0 / 12.0
MASKED_SCORE = -1e30


def passed_along(x, axis, by):
    count = lax.axis_size(axis)
    pairs = [(i, i + by) for i in range(count) if 0 <= i + by < count]
    return lax.ppermute(x, axis, pairs)


def rollout_index(finish, places):
    return jnp.sum((finish[None, :] <= places[:, None]).astype(jnp.int32), axis=1)


def visible_pairs(query_places, query_ids, key_places, key_ids):
    distance = query_places[:, None] - key_places[None, :]
    return (query_ids[:, None] == key_ids[None, :]) & (distance >= 0) & (distance < WINDOW)


def block_scores(grouped_q, key_block, visible, head_dim):
    raw = jnp.einsum(
        "tkgd,skd->kgts", grouped_q, key_block[..., :head_dim], preferred_element_type=jnp.float32
    )
    return jnp.where(visible, raw * SCORE_SCALE, MASKED_SCORE)


def gather_stats(state, grouped_q, key_block, visible, head_dim):
    run_max, run_total = state
    scores = block_scores(grouped_q, key_block, visible, head_dim)
    new_max = jnp.maximum(run_max, jnp.max(scores, axis=-1))
    weights = jnp.where(visible, jnp.exp(scores - new_max[..., None]), 0.0)
    return (new_max, run_total * jnp.exp(run_max - new_max) + jnp.sum(weights, axis=-1))


def block_probs(grouped_q, key_block, visible, log_total, head_dim):
    scores = block_scores(grouped_q, key_block, visible, head_dim)
    return jnp.where(visible, jnp.exp(scores - log_total[..., None]), 0.0)


def forward_block(total, grouped_q, key_block, visible, log_total, head_dim):
    probs_b = block_probs(grouped_q, key_block, visible, log_total, head_dim).astype(jnp.bfloat16)
    return total + jnp.einsum(
        "kgts,skd->tkgd", probs_b, key_block[..., head_dim:], preferred_element_type=jnp.float32
    )


def backward_block(grouped_q, key_block, visible, log_total, d_grouped, delta, head_dim):
    probs = block_probs(grouped_q, key_block, visible, log_total, head_dim)
    probs_b = probs.astype(jnp.bfloat16)
    d_probs = jnp.einsum(
        "tkgd,skd->kgts", d_grouped, key_block[..., head_dim:], preferred_element_type=jnp.float32
    )
    d_scores = (probs * (d_probs - delta[..., None])).astype(jnp.bfloat16)
    d_query = (
        jnp.einsum(
            "kgts,skd->tkgd",
            d_scores,
            key_block[..., :head_dim],
            preferred_element_type=jnp.float32,
        )
        * SCORE_SCALE
    )
    d_key = (
        jnp.einsum("kgts,tkgd->skd", d_scores, grouped_q, preferred_element_type=jnp.float32)
        * SCORE_SCALE
    )
    d_value = jnp.einsum("kgts,tkgd->skd", probs_b, d_grouped, preferred_element_type=jnp.float32)
    return (d_query, jnp.concatenate([d_key, d_value], axis=-1))


def keep_state(carried):
    return carried


def per_device(queries, keys, values, out_weight, cotangent, advantages, lengths):
    local_rows, local_heads, head_dim = queries.shape
    local_kv = keys.shape[1]
    group_size = local_heads // local_kv
    seq_count = lax.axis_size("seq")
    seq_index = lax.axis_index("seq")
    tp_index = lax.axis_index("tp")
    blocks_back = min(WINDOW // local_rows, seq_count - 1)
    finish = jnp.cumsum(lengths)
    offsets = jnp.arange(local_rows, dtype=jnp.int32)
    query_places = seq_index * local_rows + offsets
    query_ids = rollout_index(finish, query_places)
    packed = jnp.concatenate([keys, values], axis=-1)
    levels = [(1, number - 1, 1) for number in range(1, blocks_back + 1)]
    key_blocks = [packed]
    for distance, anchor, amount in levels:
        outgoing = jnp.stack(key_blocks[anchor : anchor + amount])
        incoming = passed_along(outgoing, "seq", distance)
        key_blocks.extend([incoming[0]])
    masks = []
    for behind in range(blocks_back + 1):
        key_places = (seq_index - behind) * local_rows + offsets
        key_ids = jnp.where(key_places >= 0, rollout_index(finish, key_places), -1)
        masks.append(visible_pairs(query_places, query_ids, key_places, key_ids))
    grouped_q = queries.reshape(local_rows, local_kv, group_size, head_dim)
    state = (
        jnp.full((local_kv, group_size, local_rows), MASKED_SCORE, jnp.float32),
        jnp.zeros((local_kv, group_size, local_rows), jnp.float32),
    )
    for behind in range(blocks_back + 1):
        update = partial(
            gather_stats,
            grouped_q=grouped_q,
            key_block=key_blocks[behind],
            visible=masks[behind],
            head_dim=head_dim,
        )
        state = lax.cond(jnp.any(masks[behind]), update, keep_state, state)
    log_total = state[0] + jnp.log(state[1])
    total = jnp.zeros((local_rows, local_kv, group_size, head_dim), jnp.float32)
    for behind in range(blocks_back + 1):
        accumulate = partial(
            forward_block,
            grouped_q=grouped_q,
            key_block=key_blocks[behind],
            visible=masks[behind],
            log_total=log_total,
            head_dim=head_dim,
        )
        total = lax.cond(jnp.any(masks[behind]), accumulate, keep_state, total)
    attention_b = total.astype(jnp.bfloat16)
    attention = attention_b.reshape(local_rows, local_heads, head_dim)
    split_rows = cotangent.shape[0]
    cot_places = (
        seq_index * local_rows + tp_index * split_rows + jnp.arange(split_rows, dtype=jnp.int32)
    )
    cot_ids = rollout_index(finish, cot_places)
    rollout_slots = jnp.arange(advantages.shape[0], dtype=jnp.int32)
    factors = jnp.sum(
        jnp.where(cot_ids[:, None] == rollout_slots[None, :], advantages[None, :], 0.0), axis=1
    )
    scaled_part = (factors[:, None] * cotangent.astype(jnp.float32)).astype(jnp.bfloat16)
    scaled = lax.all_gather(scaled_part, "tp", axis=0, tiled=True)
    d_flat = lax.dot_general(
        scaled, out_weight, (((1,), (1,)), ((), ())), preferred_element_type=jnp.float32
    ).astype(jnp.bfloat16)
    d_grouped = d_flat.reshape(local_rows, local_kv, group_size, head_dim)
    delta = jnp.transpose(
        jnp.sum(d_grouped.astype(jnp.float32) * attention_b.astype(jnp.float32), axis=-1), (1, 2, 0)
    )
    attention_flat = attention.reshape(local_rows, local_heads * head_dim)
    d_weight = lax.psum_scatter(
        lax.dot_general(
            scaled, attention_flat, (((0,), (0,)), ((), ())), preferred_element_type=jnp.float32
        ),
        "seq",
        scatter_dimension=0,
        tiled=True,
    )
    zero_query = jnp.zeros((local_rows, local_kv, group_size, head_dim), jnp.float32)
    zero_block = jnp.zeros((local_rows, local_kv, 2 * head_dim), jnp.float32)
    query_grad = zero_query
    partials = []
    for behind in range(blocks_back + 1):
        gradient_step = partial(
            backward_block,
            grouped_q=grouped_q,
            key_block=key_blocks[behind],
            visible=masks[behind],
            log_total=log_total,
            d_grouped=d_grouped,
            delta=delta,
            head_dim=head_dim,
        )
        query_part, key_grad = lax.cond(
            jnp.any(masks[behind]), gradient_step, lambda: (zero_query, zero_block)
        )
        query_grad = query_grad + query_part
        partials.append(key_grad)
    for distance, anchor, amount in reversed(levels):
        outgoing = jnp.stack(partials[anchor + distance : anchor + distance + amount])
        incoming = passed_along(outgoing, "seq", -distance)
        partials[anchor] = partials[anchor] + incoming[0]
    own_grad = partials[0]
    d_queries = query_grad.astype(jnp.bfloat16).reshape(local_rows, local_heads, head_dim)
    d_keys = own_grad[..., :head_dim].astype(jnp.bfloat16)
    d_values = own_grad[..., head_dim:].astype(jnp.bfloat16)
    return (attention, d_queries, d_keys, d_values, d_weight)


def solution(mesh):
    in_specs = (
        P("seq", "tp", None),
        P("seq", "tp", None),
        P("seq", "tp", None),
        P("tp", None),
        P(("seq", "tp"), None),
        P(),
        P(),
    )
    out_specs = (
        P("seq", "tp", None),
        P("seq", "tp", None),
        P("seq", "tp", None),
        P("seq", "tp", None),
        P("seq", "tp"),
    )
    return jax.shard_map(
        per_device, mesh=mesh, in_specs=in_specs, out_specs=out_specs, check_vma=False
    )
```

profile of v0, /device:TPU:4, one launch (start us, length us, event | category | flops | bytes accessed | tf_op | source)
XLA Modules:
  0.0 287.7 jit_solution(4616300088519464650)
XLA Ops:
  14.6 7.9 %collective-permute-done = bf16[1,512,1,256]{3,1,2,0:T(8,128)(2,1)S(1)} collective-permute-done((bf16[1,512,1,256]{3,1,2,0:T(8,128)(2,1)S(1)}, bf16[1,512,1,256]{3,1,2,0:T(8,128)(2,1)S(1)}, u32[]{:S(2)}, u32[]{:S(2)}) %collective-permute-start) | collective-permute-done | bytes 262176 | tf_op jit(solution)/shard_map/ppermute | solution.py:18
  25.5 6.7 %collective-permute-done.1 = bf16[1,512,1,256]{3,1,2,0:T(8,128)(2,1)S(1)} collective-permute-done((bf16[1,512,1,256]{3,1,2,0:T(8,128)(2,1)S(1)}, bf16[1,512,1,256]{3,1,2,0:T(8,128)(2,1)S(1)}, u32[]{:S(2)}, u32[]{:S(2)}) %collective-permute-start.1) | collective-permute-done | bytes 262176 | tf_op jit(solution)/shard_map/ppermute | solution.py:18
  35.9 6.1 %collective-permute-done.2 = bf16[1,512,1,256]{3,1,2,0:T(8,128)(2,1)S(1)} collective-permute-done((bf16[1,512,1,256]{3,1,2,0:T(8,128)(2,1)S(1)}, bf16[1,512,1,256]{3,1,2,0:T(8,128)(2,1)S(1)}, u32[]{:S(2)}, u32[]{:S(2)}) %collective-permute-start.2) | collective-permute-done | bytes 262176 | tf_op jit(solution)/shard_map/ppermute | solution.py:18
  45.4 6.5 %collective-permute-done.3 = bf16[1,512,1,256]{3,1,2,0:T(8,128)(2,1)} collective-permute-done((bf16[1,512,1,256]{3,1,2,0:T(8,128)(2,1)S(1)}, bf16[1,512,1,256]{3,1,2,0:T(8,128)(2,1)}, u32[]{:S(2)}, u32[]{:S(2)}) %collective-permute-start.3) | collective-permute-done | bytes 262176 | tf_op jit(solution)/shard_map/ppermute | solution.py:18
  53.9 8.1 %collective-permute-done.4 = bf16[1,512,1,256]{3,1,2,0:T(8,128)(2,1)S(1)} collective-permute-done((bf16[1,512,1,256]{3,1,2,0:T(8,128)(2,1)}, bf16[1,512,1,256]{3,1,2,0:T(8,128)(2,1)S(1)}, u32[]{:S(2)}, u32[]{:S(2)}) %collective-permute-start.4) | collective-permute-done | bytes 262176 | tf_op jit(solution)/shard_map/ppermute | solution.py:18
  63.9 7.8 %collective-permute-done.5 = bf16[1,512,1,256]{3,1,2,0:T(8,128)(2,1)S(1)} collective-permute-done((bf16[1,512,1,256]{3,1,2,0:T(8,128)(2,1)S(1)}, bf16[1,512,1,256]{3,1,2,0:T(8,128)(2,1)S(1)}, u32[]{:S(2)}, u32[]{:S(2)}) %collective-permute-start.5) | collective-permute-done | bytes 262176 | tf_op jit(solution)/shard_map/ppermute | solution.py:18
  73.6 6.3 %fusion.460 = (pred[512,512]{0,1:T(8,128)(4,1)S(1)}, pred[]{:T(512)}, pred[]{:T(512)}, pred[512,512]{0,1:T(8,128)(4,1)}, pred[]{:T(512)}, /*index=5*/pred[512,51...) fusion(s32[512]{0:T(512)S(1)} %iota_add_fusion.8, ...), kind=kLoop, calls=%fused_computation.553 | loop fusion | flops 14680056 | bytes 2131976 | tf_op jit(solution)/shard_map/and | solution.py:27
  100.6 2.2 conditional.32
  107.3 2.3 conditional.35
  109.7 2.9 conditional.36
  109.7 2.8 fusion.51
  112.6 3.1 %conditional.37 = (f32[512,1,2,128]{3,0,2,1:T(8,128)}) conditional(s32[]{:T(128)} %convert_element_type.214, f32[512,1,2,128]{3,0,2,1:T(8,128)} %get-tuple-element.1140, (pred[512,512]{0,1:T(8,128)(4,1)S(1)}, bf16[512,1,256]{2,0,1:T(8,128)(2,1)}, bf16[512,1,2,128]{0,3,2,1:T(8,128)(2,1)S(1)}, f32[1,2,512]{2,1,0:T(2,128)S(1)}, ...), branch_computations={%region_57.58_spmd, %region_58.59_spmd} | conditional | flops 271187968 | bytes 1839112 | solution.py:134
  112.6 3.1 %fusion.72 = f32[512,1,2,128]{3,0,2,1:T(8,128)} fusion(f32[512,1,2,128]{3,0,2,1:T(8,128)} %get-tuple-element.428, f32[2,512]{1,0:T(2,128)S(1)} %bitcast.1508, pred[512,512]{0,1:T(8,128)(4,1)S(1)} %get-tuple-element.429, bf16[512,1,2,128]{0,3,2,1:T(8,128)(2,1)S(1)} %get-tuple-element.932, bf16[512,1,256]{2,0,1:T(8,128)(2,1)} %get-tuple-element.430), kind=kOutput, calls=%fused_computation.108 | convolution fusion | flops 271187968 | bytes 1839104 | tf_op jit(solution)/shard_map/cond/branch_1_fun/kgts,skd->tkgd/dot_general | solution.py:52
  115.7 3.2 %conditional.38 = (f32[512,1,2,128]{3,0,2,1:T(8,128)}) conditional(s32[]{:T(128)} %convert_element_type.212, f32[512,1,2,128]{3,0,2,1:T(8,128)} %get-tuple-element.1141, (pred[512,512]{0,1:T(8,128)(4,1)}, bf16[512,1,256]{2,0,1:T(8,128)(2,1)}, bf16[512,1,2,128]{0,3,2,1:T(8,128)(2,1)S(1)}, f32[1,2,512]{2,1,0:T(2,128)S(1)}, ...), branch_computations={%region_59.60_spmd, %region_60.61_spmd} | conditional | flops 271187968 | bytes 1839112 | solution.py:134
  115.7 3.2 %fusion.96 = f32[512,1,2,128]{3,0,2,1:T(8,128)} fusion(f32[512,1,2,128]{3,0,2,1:T(8,128)} %get-tuple-element.433, f32[2,512]{1,0:T(2,128)S(1)} %bitcast.1509, pred[512,512]{0,1:T(8,128)(4,1)} %get-tuple-element.434, bf16[512,1,2,128]{0,3,2,1:T(8,128)(2,1)S(1)} %get-tuple-element.937, bf16[512,1,256]{2,0,1:T(8,128)(2,1)} %get-tuple-element.435), kind=kOutput, calls=%fused_computation.130 | convolution fusion | flops 271187968 | bytes 1839104 | tf_op jit(solution)/shard_map/cond/branch_1_fun/kgts,skd->tkgd/dot_general | solution.py:52
  118.9 3.1 %conditional.39 = (f32[512,1,2,128]{3,0,2,1:T(8,128)}) conditional(s32[]{:T(128)} %convert_element_type.210, f32[512,1,2,128]{3,0,2,1:T(8,128)} %get-tuple-element.1142, (pred[512,512]{0,1:T(8,128)(4,1)S(1)}, bf16[512,1,256]{2,0,1:T(8,128)(2,1)}, bf16[512,1,2,128]{0,3,2,1:T(8,128)(2,1)S(1)}, f32[1,2,512]{2,1,0:T(2,128)S(1)}, ...), branch_computations={%region_61.62_spmd, %region_62.63_spmd} | conditional | flops 271187968 | bytes 1839112 | solution.py:134
  118.9 3.1 %fusion.120 = f32[512,1,2,128]{3,0,2,1:T(8,128)} fusion(f32[512,1,2,128]{3,0,2,1:T(8,128)} %get-tuple-element.438, f32[2,512]{1,0:T(2,128)S(1)} %bitcast.1510, pred[512,512]{0,1:T(8,128)(4,1)S(1)} %get-tuple-element.439, bf16[512,1,2,128]{0,3,2,1:T(8,128)(2,1)S(1)} %get-tuple-element.942, bf16[512,1,256]{2,0,1:T(8,128)(2,1)} %get-tuple-element.440), kind=kOutput, calls=%fused_computation.152 | convolution fusion | flops 271187968 | bytes 1839104 | tf_op jit(solution)/shard_map/cond/branch_1_fun/kgts,skd->tkgd/dot_general | solution.py:52
  121.9 3.2 %conditional.40 = (f32[512,1,2,128]{3,0,2,1:T(8,128)}) conditional(s32[]{:T(128)} %convert_element_type.208, f32[512,1,2,128]{3,0,2,1:T(8,128)} %get-tuple-element.1143, (pred[512,512]{0,1:T(8,128)(4,1)}, bf16[512,1,256]{2,0,1:T(8,128)(2,1)}, bf16[512,1,2,128]{0,3,2,1:T(8,128)(2,1)S(1)}, f32[1,2,512]{2,1,0:T(2,128)S(1)}, ...), branch_computations={%region_63.64_spmd, %region_64.65_spmd} | conditional | flops 271187968 | bytes 1839112 | solution.py:134
  121.9 3.2 %fusion.144 = f32[512,1,2,128]{3,0,2,1:T(8,128)} fusion(f32[512,1,2,128]{3,0,2,1:T(8,128)} %get-tuple-element.443, f32[2,512]{1,0:T(2,128)S(1)} %bitcast.1511, pred[512,512]{0,1:T(8,128)(4,1)} %get-tuple-element.444, bf16[512,1,2,128]{0,3,2,1:T(8,128)(2,1)S(1)} %get-tuple-element.947, bf16[512,1,256]{2,0,1:T(8,128)(2,1)} %get-tuple-element.445), kind=kOutput, calls=%fused_computation.174 | convolution fusion | flops 271187968 | bytes 1839104 | tf_op jit(solution)/shard_map/cond/branch_1_fun/kgts,skd->tkgd/dot_general | solution.py:52
  125.1 3.1 %conditional.41 = (f32[512,1,2,128]{3,0,2,1:T(8,128)}) conditional(s32[]{:T(128)} %convert_element_type.206, f32[512,1,2,128]{3,0,2,1:T(8,128)} %get-tuple-element.1144, (pred[512,512]{0,1:T(8,128)(4,1)S(1)}, bf16[512,1,256]{2,0,1:T(8,128)(2,1)}, bf16[512,1,2,128]{0,3,2,1:T(8,128)(2,1)S(1)}, f32[1,2,512]{2,1,0:T(2,128)S(1)}, ...), branch_computations={%region_65.66_spmd, %region_66.67_spmd} | conditional | flops 271187968 | bytes 1839112 | solution.py:134
  125.1 3.1 %fusion.168 = f32[512,1,2,128]{3,0,2,1:T(8,128)} fusion(f32[512,1,2,128]{3,0,2,1:T(8,128)} %get-tuple-element.448, f32[2,512]{1,0:T(2,128)S(1)} %bitcast.1512, pred[512,512]{0,1:T(8,128)(4,1)S(1)} %get-tuple-element.449, bf16[512,1,2,128]{0,3,2,1:T(8,128)(2,1)S(1)} %get-tuple-element.952, bf16[512,1,256]{2,0,1:T(8,128)(2,1)} %get-tuple-element.450), kind=kOutput, calls=%fused_computation.196 | convolution fusion | flops 271187968 | bytes 1839104 | tf_op jit(solution)/shard_map/cond/branch_1_fun/kgts,skd->tkgd/dot_general | solution.py:52
  128.2 3.2 %conditional.42 = (f32[512,1,2,128]{3,0,2,1:T(8,128)}) conditional(s32[]{:T(128)} %convert_element_type.204, f32[512,1,2,128]{3,0,2,1:T(8,128)} %get-tuple-element.1145, (pred[512,512]{0,1:T(8,128)(4,1)}, bf16[512,1,256]{2,0,1:T(8,128)(2,1)}, bf16[512,1,2,128]{0,3,2,1:T(8,128)(2,1)S(1)}, f32[1,2,512]{2,1,0:T(2,128)S(1)}, ...), branch_computations={%region_67.68_spmd, %region_68.69_spmd} | conditional | flops 271187968 | bytes 1839112 | solution.py:134
  128.2 3.2 %fusion.192 = f32[512,1,2,128]{3,0,2,1:T(8,128)} fusion(f32[512,1,2,128]{3,0,2,1:T(8,128)} %get-tuple-element.453, f32[2,512]{1,0:T(2,128)S(1)} %bitcast.1513, pred[512,512]{0,1:T(8,128)(4,1)} %get-tuple-element.454, bf16[512,1,2,128]{0,3,2,1:T(8,128)(2,1)S(1)} %get-tuple-element.957, bf16[512,1,256]{2,0,1:T(8,128)(2,1)} %get-tuple-element.455), kind=kOutput, calls=%fused_computation.218 | convolution fusion | flops 271187968 | bytes 1839104 | tf_op jit(solution)/shard_map/cond/branch_1_fun/kgts,skd->tkgd/dot_general | solution.py:52
  131.4 3.1 %conditional.43 = (f32[512,1,2,128]{3,0,2,1:T(8,128)}) conditional(s32[]{:T(128)} %convert_element_type.202, f32[512,1,2,128]{3,0,2,1:T(8,128)} %get-tuple-element.1146, (pred[512,512]{0,1:T(8,128)(4,1)S(1)}, bf16[512,1,256]{2,0,1:T(8,128)(2,1)}, bf16[512,1,2,128]{0,3,2,1:T(8,128)(2,1)S(1)}, f32[1,2,512]{2,1,0:T(2,128)S(1)}, ...), branch_computations={%region_69.70_spmd, %region_70.71_spmd} | conditional | flops 271187968 | bytes 1839112 | solution.py:134
  131.4 3.1 %fusion.216 = f32[512,1,2,128]{3,0,2,1:T(8,128)} fusion(f32[512,1,2,128]{3,0,2,1:T(8,128)} %get-tuple-element.458, f32[2,512]{1,0:T(2,128)S(1)} %bitcast.1514, pred[512,512]{0,1:T(8,128)(4,1)S(1)} %get-tuple-element.459, bf16[512,1,2,128]{0,3,2,1:T(8,128)(2,1)S(1)} %get-tuple-element.962, bf16[512,1,256]{2,0,1:T(8,128)(2,1)} %get-tuple-element.460), kind=kOutput, calls=%fused_computation.240 | convolution fusion | flops 271187968 | bytes 1839104 | tf_op jit(solution)/shard_map/cond/branch_1_fun/kgts,skd->tkgd/dot_general | solution.py:52
  134.5 3.5 %conditional.54 = (f32[512,1,2,128]{3,0,2,1:T(8,128)}) conditional(s32[]{:T(128)} %convert_element_type.200, f32[512,1,2,128]{3,0,2,1:T(8,128)} %get-tuple-element.1147, (pred[512,512]{0,1:T(8,128)(4,1)S(1)}, bf16[512,1,256]{2,0,1:T(8,128)(2,1)}, bf16[512,1,2,128]{0,3,2,1:T(8,128)(2,1)S(1)}, f32[1,2,512]{2,1,0:T(2,128)S(1)}, ...), branch_computations={%region_71.72_spmd.clone, %region_72.73_spmd.clone} | conditional | flops 271187968 | bytes 1839112
  134.5 3.1 %fusion.426 = f32[512,1,2,128]{3,0,2,1:T(8,128)} fusion(f32[512,1,2,128]{3,0,2,1:T(8,128)} %get-tuple-element.612, f32[2,512]{1,0:T(2,128)S(1)} %bitcast.1515, pred[512,512]{0,1:T(8,128)(4,1)S(1)} %get-tuple-element.613, bf16[512,1,2,128]{0,3,2,1:T(8,128)(2,1)S(1)} %get-tuple-element.967, bf16[512,1,256]{2,0,1:T(8,128)(2,1)} %get-tuple-element.614), kind=kOutput, calls=%fused_computation.502 | convolution fusion | flops 271187968 | bytes 1839104 | tf_op jit(solution)/shard_map/cond/branch_1_fun/kgts,skd->tkgd/dot_general | solution.py:52
  139.3 6.0 %fusion.489 = f32[4608,256]{1,0:T(8,128)} fusion(bf16[512,4608]{1,0:T(8,128)(2,1)} %all-gather.2.cloned.1.call-done, bf16[512,256]{0,1:T(8,128)(2,1)S(1)} %bitcast.1464), kind=kOutput, calls=%fused_computation.617 | convolution fusion | flops 1207959552 | bytes 9699328 | tf_op jit(solution)/shard_map/dot_general | solution.py:157
  145.3 3.8 %convolution_convert_fusion = bf16[512,256]{0,1:T(8,128)(2,1)S(1)} fusion(bf16[512,4608]{1,0:T(8,128)(2,1)} %all-gather.2.cloned.1.call-done, bf16[256,4608]{1,0:T(8,128)(2,1)S(1)} %copy-done), kind=kOutput, calls=%fused_computation.534 | convolution fusion | flops 1208090624 | bytes 7340032 | tf_op jit(solution)/shard_map/dot_general | solution.py:148
  149.3 6.3 %conditional.53 = (f32[512,1,2,128]{3,0,2,1:T(8,128)}, f32[512,1,256]{0,2,1:T(8,128)S(1)}) conditional(s32[]{:T(128)} %convert_element_type.200, () %tuple.252, (pred[512,512]{0,1:T(8,128)(4,1)S(1)}, bf16[512,1,256]{2,0,1:T(8,128)(2,1)}, bf16[512,1,2,128]{0,3,2,1:T(8,128)(2,1)S(1)}, f32[1,2,512]{2,1,0:T(2,128)S(1)}, ...), branch_computations={%region_92.93_spmd, %region_93.94_spmd} | conditional | flops 675610624 | bytes 13246480 | solution.py:179
  158.5 5.7 %conditional.52 = (f32[512,1,2,128]{3,0,2,1:T(8,128)S(1)}, f32[512,1,256]{2,0,1:T(8,128)S(1)}) conditional(s32[]{:T(128)} %convert_element_type.202, () %tuple.250, (pred[512,512]{0,1:T(8,128)(4,1)S(1)}, bf16[512,1,256]{2,0,1:T(8,128)(2,1)}, bf16[512,1,2,128]{0,3,2,1:T(8,128)(2,1)S(1)}, f32[1,2,512]{2,1,0:T(2,128)S(1)}, ...), branch_computations={%region_90.91_spmd, %region_91.92_spmd} | conditional | flops 675610624 | bytes 14295056 | solution.py:179
  167.4 5.9 %collective-permute-start.9 = (f32[1,512,1,256]{3,1,2,0:T(8,128)}, f32[1,512,1,256]{3,1,2,0:T(8,128)}, u32[]{:S(2)}, u32[]{:S(2)}) collective-permute-start(f32[1,512,1,256]{3,1,2,0:T(8,128)} %fusion.468), channel_id=1, source_target_pairs={{8,0},{16,8},{24,16},{32,24},{40,32},{48,40},{56,48},{64,56},{72,6... | collective-permute-start | bytes 1572872 | tf_op jit(solution)/shard_map/ppermute | solution.py:18
  173.3 5.6 %conditional.51 = (f32[512,1,2,128]{3,0,2,1:T(8,128)S(1)}, f32[512,1,256]{2,0,1:T(8,128)}) conditional(s32[]{:T(128)} %convert_element_type.204, () %tuple.248, (pred[512,512]{0,1:T(8,128)(4,1)S(1)}, bf16[512,1,256]{2,0,1:T(8,128)(2,1)}, bf16[512,1,2,128]{0,3,2,1:T(8,128)(2,1)S(1)}, f32[1,2,512]{2,1,0:T(2,128)S(1)}, ...), branch_computations={%region_88.89_spmd, %region_89.90_spmd} | conditional | flops 675610624 | bytes 15343660 | solution.py:179
  182.4 5.9 %collective-permute-start.10 = (f32[1,512,1,256]{3,1,2,0:T(8,128)}, f32[1,512,1,256]{3,1,2,0:T(8,128)}, u32[]{:S(2)}, u32[]{:S(2)}) collective-permute-start(f32[1,512,1,256]{3,1,2,0:T(8,128)} %fusion.467), channel_id=1, source_target_pairs={{8,0},{16,8},{24,16},{32,24},{40,32},{48,40},{56,48},{64,56},{72,6... | collective-permute-start | bytes 1572872 | tf_op jit(solution)/shard_map/ppermute | solution.py:18
  188.3 5.9 %conditional.50 = (f32[512,1,2,128]{3,0,2,1:T(8,128)S(1)}, f32[512,1,256]{2,0,1:T(8,128)}) conditional(s32[]{:T(128)} %convert_element_type.206, () %tuple.246, (pred[512,512]{0,1:T(8,128)(4,1)}, bf16[512,1,256]{2,0,1:T(8,128)(2,1)}, bf16[512,1,2,128]{0,3,2,1:T(8,128)(2,1)S(1)}, f32[1,2,512]{2,1,0:T(2,128)S(1)}, ...), branch_computations={%region_86.87_spmd, %region_87.88_spmd} | conditional | flops 675610624 | bytes 15343660 | solution.py:179
  197.3 5.9 %collective-permute-start.11 = (f32[1,512,1,256]{3,1,2,0:T(8,128)}, f32[1,512,1,256]{3,1,2,0:T(8,128)}, u32[]{:S(2)}, u32[]{:S(2)}) collective-permute-start(f32[1,512,1,256]{3,1,2,0:T(8,128)} %fusion.466), channel_id=1, source_target_pairs={{8,0},{16,8},{24,16},{32,24},{40,32},{48,40},{56,48},{64,56},{72,6... | collective-permute-start | bytes 1572872 | tf_op jit(solution)/shard_map/ppermute | solution.py:18
  203.3 6.6 %conditional.49 = (f32[512,1,2,128]{3,0,2,1:T(8,128)S(1)}, f32[512,1,256]{2,0,1:T(8,128)}) conditional(s32[]{:T(128)} %convert_element_type.208, () %tuple.244, (pred[512,512]{0,1:T(8,128)(4,1)}, bf16[512,1,256]{2,0,1:T(8,128)(2,1)}, bf16[512,1,2,128]{0,3,2,1:T(8,128)(2,1)S(1)}, f32[1,2,512]{2,1,0:T(2,128)S(1)}, ...), branch_computations={%region_84.85_spmd, %region_85.86_spmd} | conditional | flops 675610624 | bytes 14295056 | solution.py:179
  209.9 5.6 %collective-permute-done.11 = f32[1,512,1,256]{3,1,2,0:T(8,128)} collective-permute-done((f32[1,512,1,256]{3,1,2,0:T(8,128)}, f32[1,512,1,256]{3,1,2,0:T(8,128)}, u32[]{:S(2)}, u32[]{:S(2)}) %collective-permute-start.11) | collective-permute-done | bytes 524320 | tf_op jit(solution)/shard_map/ppermute | solution.py:18
  217.6 5.9 %collective-permute-start.12 = (f32[1,512,1,256]{3,1,2,0:T(8,128)}, f32[1,512,1,256]{3,1,2,0:T(8,128)}, u32[]{:S(2)}, u32[]{:S(2)}) collective-permute-start(f32[1,512,1,256]{3,1,2,0:T(8,128)} %fusion.465), channel_id=1, source_target_pairs={{8,0},{16,8},{24,16},{32,24},{40,32},{48,40},{56,48},{64,56},{72,6... | collective-permute-start | bytes 1572872 | tf_op jit(solution)/shard_map/ppermute | solution.py:18
  223.5 4.8 %conditional.48 = (f32[512,1,2,128]{3,0,2,1:T(8,128)S(1)}, f32[512,1,256]{2,0,1:T(8,128)}) conditional(s32[]{:T(128)} %convert_element_type.210, () %tuple.242, (pred[512,512]{0,1:T(8,128)(4,1)}, bf16[512,1,256]{2,0,1:T(8,128)(2,1)}, bf16[512,1,2,128]{0,3,2,1:T(8,128)(2,1)S(1)}, f32[1,2,512]{2,1,0:T(2,128)S(1)}, ...), branch_computations={%region_82.83_spmd, %region_83.84_spmd} | conditional | flops 675610624 | bytes 15343660 | solution.py:179
  228.3 3.1 %collective-permute-done.12 = f32[1,512,1,256]{3,1,2,0:T(8,128)} collective-permute-done((f32[1,512,1,256]{3,1,2,0:T(8,128)}, f32[1,512,1,256]{3,1,2,0:T(8,128)}, u32[]{:S(2)}, u32[]{:S(2)}) %collective-permute-start.12) | collective-permute-done | bytes 524320 | tf_op jit(solution)/shard_map/ppermute | solution.py:18
  233.6 5.9 %collective-permute-start.13 = (f32[1,512,1,256]{3,1,2,0:T(8,128)}, f32[1,512,1,256]{3,1,2,0:T(8,128)}, u32[]{:S(2)}, u32[]{:S(2)}) collective-permute-start(f32[1,512,1,256]{3,1,2,0:T(8,128)} %fusion.464), channel_id=1, source_target_pairs={{8,0},{16,8},{24,16},{32,24},{40,32},{48,40},{56,48},{64,56},{72,6... | collective-permute-start | bytes 1572872 | tf_op jit(solution)/shard_map/ppermute | solution.py:18
  239.5 5.7 %conditional.47 = (f32[512,1,2,128]{3,0,2,1:T(8,128)S(1)}, f32[512,1,256]{2,0,1:T(8,128)}) conditional(s32[]{:T(128)} %convert_element_type.212, () %tuple.240, (pred[512,512]{0,1:T(8,128)(4,1)}, bf16[512,1,256]{2,0,1:T(8,128)(2,1)}, bf16[512,1,2,128]{0,3,2,1:T(8,128)(2,1)S(1)}, f32[1,2,512]{2,1,0:T(2,128)S(1)}, ...), branch_computations={%region_80.81_spmd, %region_81.82_spmd} | conditional | flops 675610624 | bytes 15343660 | solution.py:179
  248.6 5.9 %collective-permute-start.14 = (f32[1,512,1,256]{3,1,2,0:T(8,128)}, f32[1,512,1,256]{3,1,2,0:T(8,128)}, u32[]{:S(2)}, u32[]{:S(2)}) collective-permute-start(f32[1,512,1,256]{3,1,2,0:T(8,128)} %fusion.463), channel_id=1, source_target_pairs={{8,0},{16,8},{24,16},{32,24},{40,32},{48,40},{56,48},{64,56},{72,6... | collective-permute-start | bytes 1572872 | tf_op jit(solution)/shard_map/ppermute | solution.py:18
  254.5 4.9 %conditional.46 = (f32[512,1,2,128]{3,0,2,1:T(8,128)S(1)}, f32[512,1,256]{2,0,1:T(8,128)}) conditional(s32[]{:T(128)} %convert_element_type.214, () %tuple.238, (pred[512,512]{0,1:T(8,128)(4,1)S(1)}, bf16[512,1,256]{2,0,1:T(8,128)(2,1)}, bf16[512,1,2,128]{0,3,2,1:T(8,128)(2,1)S(1)}, f32[1,2,512]{2,1,0:T(2,128)S(1)}, ...), branch_computations={%region_78.79_spmd, %region_79.80_spmd} | conditional | flops 675610624 | bytes 16392264 | solution.py:179
  263.6 5.9 %collective-permute-start.15 = (f32[1,512,1,256]{3,1,2,0:T(8,128)}, f32[1,512,1,256]{3,1,2,0:T(8,128)}, u32[]{:S(2)}, u32[]{:S(2)}) collective-permute-start(f32[1,512,1,256]{3,1,2,0:T(8,128)} %fusion.462), channel_id=1, source_target_pairs={{8,0},{16,8},{24,16},{32,24},{40,32},{48,40},{56,48},{64,56},{72,6... | collective-permute-start | bytes 1572872 | tf_op jit(solution)/shard_map/ppermute | solution.py:18
  270.5 4.5 %conditional.45 = (f32[512,1,2,128]{3,0,2,1:T(8,128)}, f32[512,1,256]{2,0,1:T(8,128)}) conditional(s32[]{:T(128)} %convert_element_type.215, () %tuple.236, (pred[512,512]{0,1:T(8,128)(4,1)S(1)}, bf16[512,1,128]{2,0,1:T(8,128)(2,1)S(1)}, bf16[512,1,2,128]{0,3,2,1:T(8,128)(2,1)S(1)}, f32[1,2,512]{2,1,0:T(2,128)S(1)}, ...), branch_computations={%region_76.77_spmd, %region_77.78_spmd} | conditional | flops 675610624 | bytes 14295056 | solution.py:179
  275.0 2.7 fusion.469
  (259 shorter events, 139.6 us)
Async XLA Ops:
  7.2 138.1 %copy-start = (bf16[256,4608]{1,0:T(8,128)(2,1)S(1)}, bf16[256,4608]{1,0:T(8,128)(2,1)}, u32[]{:S(2)}) copy-start(bf16[256,4608]{1,0:T(8,128)(2,1)} %param.64) | copy-start | bytes 7077892
  7.2 132.1 %all-gather.2.cloned.1.call-start = ((), (), s32[]{:S(2)}) async-start(), calls=%async_computation.1 | async-start | bytes 5308416 | tf_op jit(solution)/shard_map/all_gather | solution.py:147
  9.5 74.1 %copy-start.29 = (bf16[512,2,128]{2,1,0:T(2,128)(2,1)S(1)}, bf16[512,2,128]{2,1,0:T(2,128)(2,1)}, u32[]{:S(2)}) copy-start(bf16[512,2,128]{2,1,0:T(2,128)(2,1)} %param.61) | copy-start | bytes 786436
  11.6 78.9 %copy-start.11 = (bf16[512,1,128]{2,0,1:T(8,128)(2,1)S(1)}, bf16[512,1,128]{2,0,1:T(8,128)(2,1)}, u32[]{:S(2)}) copy-start(bf16[512,1,128]{2,0,1:T(8,128)(2,1)} %param.62) | copy-start | bytes 393220
  11.6 269.0 %reduce-scatter.2.cloned.1.call-start = ((), (), s32[]{:S(2)}) async-start(), calls=%async_computation.2 | async-start | bytes 4866048 | tf_op jit(solution)/shard_map/reduce_scatter | solution.py:156
  12.6 9.8 %collective-permute-start = (bf16[1,512,1,256]{3,1,2,0:T(8,128)(2,1)S(1)}, bf16[1,512,1,256]{3,1,2,0:T(8,128)(2,1)S(1)}, u32[]{:S(2)}, u32[]{:S(2)}) collective-permute-start(bf16[1,512,1,256]{3,1,2,0:T(8,128)(2,1)S(1)} %maximum_bitcast_fusion), channel_id=1, source_target_pairs={{0,8},{8,16},{16,24},{24,32},{32,40},{40,48},{48,56},{56,64},{64,7... | collective-permute-start | bytes 786440 | tf_op jit(solution)/shard_map/ppermute | solution.py:18
  22.4 65.6 %copy-start.30 = (bf16[1,512,1,256]{3,1,2,0:T(8,128)(2,1)}, bf16[1,512,1,256]{3,1,2,0:T(8,128)(2,1)S(1)}, u32[]{:S(2)}) copy-start(bf16[1,512,1,256]{3,1,2,0:T(8,128)(2,1)S(1)} %collective-permute-done) | copy-start | bytes 786436
  22.4 9.8 %collective-permute-start.1 = (bf16[1,512,1,256]{3,1,2,0:T(8,128)(2,1)S(1)}, bf16[1,512,1,256]{3,1,2,0:T(8,128)(2,1)S(1)}, u32[]{:S(2)}, u32[]{:S(2)}) collective-permute-start(bf16[1,512,1,256]{3,1,2,0:T(8,128)(2,1)S(1)} %collective-permute-done), channel_id=1, source_target_pairs={{0,8},{8,16},{16,24},{24,32},{32,40},{40,48},{48,56},{56,64},{64,7... | collective-permute-start | bytes 786440 | tf_op jit(solution)/shard_map/ppermute | solution.py:18
  32.2 51.3 %copy-start.33 = (bf16[1,512,1,256]{3,1,2,0:T(8,128)(2,1)}, bf16[1,512,1,256]{3,1,2,0:T(8,128)(2,1)S(1)}, u32[]{:S(2)}) copy-start(bf16[1,512,1,256]{3,1,2,0:T(8,128)(2,1)S(1)} %collective-permute-done.1) | copy-start | bytes 786436
  32.2 9.8 %collective-permute-start.2 = (bf16[1,512,1,256]{3,1,2,0:T(8,128)(2,1)S(1)}, bf16[1,512,1,256]{3,1,2,0:T(8,128)(2,1)S(1)}, u32[]{:S(2)}, u32[]{:S(2)}) collective-permute-start(bf16[1,512,1,256]{3,1,2,0:T(8,128)(2,1)S(1)} %collective-permute-done.1), channel_id=1, source_target_pairs={{0,8},{8,16},{16,24},{24,32},{32,40},{40,48},{48,56},{56,64},{64,7... | collective-permute-start | bytes 786440 | tf_op jit(solution)/shard_map/ppermute | solution.py:18
  42.0 31.6 %copy-start.35 = (bf16[1,512,1,256]{3,1,2,0:T(8,128)(2,1)}, bf16[1,512,1,256]{3,1,2,0:T(8,128)(2,1)S(1)}, u32[]{:S(2)}) copy-start(bf16[1,512,1,256]{3,1,2,0:T(8,128)(2,1)S(1)} %collective-permute-done.2) | copy-start | bytes 786436
  42.0 9.9 %collective-permute-start.3 = (bf16[1,512,1,256]{3,1,2,0:T(8,128)(2,1)S(1)}, bf16[1,512,1,256]{3,1,2,0:T(8,128)(2,1)}, u32[]{:S(2)}, u32[]{:S(2)}) collective-permute-start(bf16[1,512,1,256]{3,1,2,0:T(8,128)(2,1)S(1)} %collective-permute-done.2), channel_id=1, source_target_pairs={{0,8},{8,16},{16,24},{24,32},{32,40},{40,48},{48,56},{56,64},{64,7... | collective-permute-start | bytes 786440 | tf_op jit(solution)/shard_map/ppermute | solution.py:18
  51.9 10.0 %collective-permute-start.4 = (bf16[1,512,1,256]{3,1,2,0:T(8,128)(2,1)}, bf16[1,512,1,256]{3,1,2,0:T(8,128)(2,1)S(1)}, u32[]{:S(2)}, u32[]{:S(2)}) collective-permute-start(bf16[1,512,1,256]{3,1,2,0:T(8,128)(2,1)} %collective-permute-done.3), channel_id=1, source_target_pairs={{0,8},{8,16},{16,24},{24,32},{32,40},{40,48},{48,56},{56,64},{64,7... | collective-permute-start | bytes 786440 | tf_op jit(solution)/shard_map/ppermute | solution.py:18
  61.9 21.6 %copy-start.37 = (bf16[1,512,1,256]{3,1,2,0:T(8,128)(2,1)}, bf16[1,512,1,256]{3,1,2,0:T(8,128)(2,1)S(1)}, u32[]{:S(2)}) copy-start(bf16[1,512,1,256]{3,1,2,0:T(8,128)(2,1)S(1)} %collective-permute-done.4) | copy-start | bytes 786436
  61.9 9.8 %collective-permute-start.5 = (bf16[1,512,1,256]{3,1,2,0:T(8,128)(2,1)S(1)}, bf16[1,512,1,256]{3,1,2,0:T(8,128)(2,1)S(1)}, u32[]{:S(2)}, u32[]{:S(2)}) collective-permute-start(bf16[1,512,1,256]{3,1,2,0:T(8,128)(2,1)S(1)} %collective-permute-done.4), channel_id=1, source_target_pairs={{0,8},{8,16},{16,24},{24,32},{32,40},{40,48},{48,56},{56,64},{64,7... | collective-permute-start | bytes 786440 | tf_op jit(solution)/shard_map/ppermute | solution.py:18
  71.7 11.9 %copy-start.39 = (bf16[1,512,1,256]{3,1,2,0:T(8,128)(2,1)}, bf16[1,512,1,256]{3,1,2,0:T(8,128)(2,1)S(1)}, u32[]{:S(2)}) copy-start(bf16[1,512,1,256]{3,1,2,0:T(8,128)(2,1)S(1)} %collective-permute-done.5) | copy-start | bytes 786436
  71.7 9.9 %collective-permute-start.6 = (bf16[1,512,1,256]{3,1,2,0:T(8,128)(2,1)S(1)}, bf16[1,512,1,256]{3,1,2,0:T(8,128)(2,1)}, u32[]{:S(2)}, u32[]{:S(2)}) collective-permute-start(bf16[1,512,1,256]{3,1,2,0:T(8,128)(2,1)S(1)} %collective-permute-done.5), channel_id=1, source_target_pairs={{0,8},{8,16},{16,24},{24,32},{32,40},{40,48},{48,56},{56,64},{64,7... | collective-permute-start | bytes 786440 | tf_op jit(solution)/shard_map/ppermute | solution.py:18
  81.6 25.7 %collective-permute-start.7 = (bf16[1,512,1,256]{3,1,2,0:T(8,128)(2,1)}, bf16[1,512,1,256]{3,1,2,0:T(8,128)(2,1)}, u32[]{:S(2)}, u32[]{:S(2)}) collective-permute-start(bf16[1,512,1,256]{3,1,2,0:T(8,128)(2,1)} %collective-permute-done.6), channel_id=1, source_target_pairs={{0,8},{8,16},{16,24},{24,32},{32,40},{40,48},{48,56},{56,64},{64,7... | collective-permute-start | bytes 786440 | tf_op jit(solution)/shard_map/ppermute | solution.py:18
  89.8 44.7 %copy-start.12 = (pred[512,512]{0,1:T(8,128)(4,1)}, pred[512,512]{0,1:T(8,128)(4,1)S(1)}, u32[]{:S(2)}) copy-start(pred[512,512]{0,1:T(8,128)(4,1)S(1)} %get-tuple-element.1013) | copy-start | bytes 786436
  109.7 2.9 copy-start.14
  115.7 3.2 %copy-start.18 = (pred[512,512]{0,1:T(8,128)(4,1)S(1)}, pred[512,512]{0,1:T(8,128)(4,1)}, u32[]{:S(2)}) copy-start(pred[512,512]{0,1:T(8,128)(4,1)} %get-tuple-element.1043) | copy-start | bytes 786436
  121.9 3.2 %copy-start.21 = (pred[512,512]{0,1:T(8,128)(4,1)S(1)}, pred[512,512]{0,1:T(8,128)(4,1)}, u32[]{:S(2)}) copy-start(pred[512,512]{0,1:T(8,128)(4,1)} %get-tuple-element.1039) | copy-start | bytes 786436
  128.2 3.2 %copy-start.25 = (pred[512,512]{0,1:T(8,128)(4,1)S(1)}, pred[512,512]{0,1:T(8,128)(4,1)}, u32[]{:S(2)}) copy-start(pred[512,512]{0,1:T(8,128)(4,1)} %get-tuple-element.1049) | copy-start | bytes 786436
  139.3 6.0 %copy-start.2 = (bf16[512,1,2,128]{0,3,2,1:T(8,128)(2,1)}, bf16[512,1,2,128]{0,3,2,1:T(8,128)(2,1)S(1)}, u32[]{:S(2)}) copy-start(bf16[512,1,2,128]{0,3,2,1:T(8,128)(2,1)S(1)} %copy.367) | copy-start | bytes 786436
  145.3 3.8 %copy-start.3 = (bf16[512,1,2,128]{0,3,2,1:T(8,128)(2,1)S(1)}, bf16[512,1,2,128]{0,3,2,1:T(8,128)(2,1)}, u32[]{:S(2)}) copy-start(bf16[512,1,2,128]{0,3,2,1:T(8,128)(2,1)} %copy-done.2) | copy-start | bytes 786436
  145.3 3.9 %copy-start.13 = (pred[512,512]{0,1:T(8,128)(4,1)S(1)}, pred[512,512]{0,1:T(8,128)(4,1)}, u32[]{:S(2)}) copy-start(pred[512,512]{0,1:T(8,128)(4,1)} %copy-done.12) | copy-start | bytes 786436
  149.3 9.2 %copy-start.26 = (pred[512,512]{0,1:T(8,128)(4,1)S(1)}, pred[512,512]{0,1:T(8,128)(4,1)}, u32[]{:S(2)}) copy-start(pred[512,512]{0,1:T(8,128)(4,1)} %get-tuple-element.1049) | copy-start | bytes 786436
  156.5 8.9 %collective-permute-start.8 = (f32[1,512,1,256]{3,1,2,0:T(8,128)}, f32[1,512,1,256]{3,1,2,0:T(8,128)}, u32[]{:S(2)}, u32[]{:S(2)}) collective-permute-start(f32[1,512,1,256]{3,1,2,0:T(8,128)} %bitcast.410), channel_id=1, source_target_pairs={{8,0},{16,8},{24,16},{32,24},{40,32},{48,40},{56,48},{64,56},{72,6... | collective-permute-start | bytes 1572872 | tf_op jit(solution)/shard_map/ppermute | solution.py:18
  158.4 14.8 %copy-start.23 = (pred[512,512]{0,1:T(8,128)(4,1)S(1)}, pred[512,512]{0,1:T(8,128)(4,1)}, u32[]{:S(2)}) copy-start(pred[512,512]{0,1:T(8,128)(4,1)} %get-tuple-element.1037) | copy-start | bytes 786436
  164.1 9.2 %copy-start.4 = (f32[512,1,2,128]{3,0,2,1:T(8,128)}, f32[512,1,2,128]{3,0,2,1:T(8,128)S(1)}, u32[]{:S(2)}) copy-start(f32[512,1,2,128]{3,0,2,1:T(8,128)S(1)} %get-tuple-element.594) | copy-start | bytes 1572868
  167.4 12.9 %collective-permute-start.9 = (f32[1,512,1,256]{3,1,2,0:T(8,128)}, f32[1,512,1,256]{3,1,2,0:T(8,128)}, u32[]{:S(2)}, u32[]{:S(2)}) collective-permute-start(f32[1,512,1,256]{3,1,2,0:T(8,128)} %fusion.468), channel_id=1, source_target_pairs={{8,0},{16,8},{24,16},{32,24},{40,32},{48,40},{56,48},{64,56},{72,6... | collective-permute-start | bytes 1572872 | tf_op jit(solution)/shard_map/ppermute | solution.py:18
  178.9 9.4 %copy-start.5 = (f32[512,1,2,128]{3,0,2,1:T(8,128)}, f32[512,1,2,128]{3,0,2,1:T(8,128)S(1)}, u32[]{:S(2)}) copy-start(f32[512,1,2,128]{3,0,2,1:T(8,128)S(1)} %get-tuple-element.593) | copy-start | bytes 1572868
  182.4 12.9 %collective-permute-start.10 = (f32[1,512,1,256]{3,1,2,0:T(8,128)}, f32[1,512,1,256]{3,1,2,0:T(8,128)}, u32[]{:S(2)}, u32[]{:S(2)}) collective-permute-start(f32[1,512,1,256]{3,1,2,0:T(8,128)} %fusion.467), channel_id=1, source_target_pairs={{8,0},{16,8},{24,16},{32,24},{40,32},{48,40},{56,48},{64,56},{72,6... | collective-permute-start | bytes 1572872 | tf_op jit(solution)/shard_map/ppermute | solution.py:18
  188.5 1.8 copy-start.38
  194.2 9.1 %copy-start.6 = (f32[512,1,2,128]{3,0,2,1:T(8,128)}, f32[512,1,2,128]{3,0,2,1:T(8,128)S(1)}, u32[]{:S(2)}) copy-start(f32[512,1,2,128]{3,0,2,1:T(8,128)S(1)} %get-tuple-element.592) | copy-start | bytes 1572868
  197.3 18.2 %collective-permute-start.11 = (f32[1,512,1,256]{3,1,2,0:T(8,128)}, f32[1,512,1,256]{3,1,2,0:T(8,128)}, u32[]{:S(2)}, u32[]{:S(2)}) collective-permute-start(f32[1,512,1,256]{3,1,2,0:T(8,128)} %fusion.466), channel_id=1, source_target_pairs={{8,0},{16,8},{24,16},{32,24},{40,32},{48,40},{56,48},{64,56},{72,6... | collective-permute-start | bytes 1572872 | tf_op jit(solution)/shard_map/ppermute | solution.py:18
  209.8 13.6 %copy-start.7 = (f32[512,1,2,128]{3,0,2,1:T(8,128)}, f32[512,1,2,128]{3,0,2,1:T(8,128)S(1)}, u32[]{:S(2)}) copy-start(f32[512,1,2,128]{3,0,2,1:T(8,128)S(1)} %get-tuple-element.591) | copy-start | bytes 1572868
  217.6 13.9 %collective-permute-start.12 = (f32[1,512,1,256]{3,1,2,0:T(8,128)}, f32[1,512,1,256]{3,1,2,0:T(8,128)}, u32[]{:S(2)}, u32[]{:S(2)}) collective-permute-start(f32[1,512,1,256]{3,1,2,0:T(8,128)} %fusion.465), channel_id=1, source_target_pairs={{8,0},{16,8},{24,16},{32,24},{40,32},{48,40},{56,48},{64,56},{72,6... | collective-permute-start | bytes 1572872 | tf_op jit(solution)/shard_map/ppermute | solution.py:18
  228.3 11.2 %copy-start.8 = (f32[512,1,2,128]{3,0,2,1:T(8,128)}, f32[512,1,2,128]{3,0,2,1:T(8,128)S(1)}, u32[]{:S(2)}) copy-start(f32[512,1,2,128]{3,0,2,1:T(8,128)S(1)} %get-tuple-element.590) | copy-start | bytes 1572868
  233.6 12.9 %collective-permute-start.13 = (f32[1,512,1,256]{3,1,2,0:T(8,128)}, f32[1,512,1,256]{3,1,2,0:T(8,128)}, u32[]{:S(2)}, u32[]{:S(2)}) collective-permute-start(f32[1,512,1,256]{3,1,2,0:T(8,128)} %fusion.464), channel_id=1, source_target_pairs={{8,0},{16,8},{24,16},{32,24},{40,32},{48,40},{56,48},{64,56},{72,6... | collective-permute-start | bytes 1572872 | tf_op jit(solution)/shard_map/ppermute | solution.py:18
  239.5 15.0 %copy-start.15 = (pred[512,512]{0,1:T(8,128)(4,1)S(1)}, pred[512,512]{0,1:T(8,128)(4,1)}, u32[]{:S(2)}) copy-start(pred[512,512]{0,1:T(8,128)(4,1)} %get-tuple-element.1047) | copy-start | bytes 786436
  239.5 1.8 copy-start.34
  245.2 9.3 %copy-start.9 = (f32[512,1,2,128]{3,0,2,1:T(8,128)}, f32[512,1,2,128]{3,0,2,1:T(8,128)S(1)}, u32[]{:S(2)}) copy-start(f32[512,1,2,128]{3,0,2,1:T(8,128)S(1)} %get-tuple-element.589) | copy-start | bytes 1572868
  248.6 12.9 %collective-permute-start.14 = (f32[1,512,1,256]{3,1,2,0:T(8,128)}, f32[1,512,1,256]{3,1,2,0:T(8,128)}, u32[]{:S(2)}, u32[]{:S(2)}) collective-permute-start(f32[1,512,1,256]{3,1,2,0:T(8,128)} %fusion.463), channel_id=1, source_target_pairs={{8,0},{16,8},{24,16},{32,24},{40,32},{48,40},{56,48},{64,56},{72,6... | collective-permute-start | bytes 1572872 | tf_op jit(solution)/shard_map/ppermute | solution.py:18
  259.5 11.1 %copy-start.10 = (f32[512,1,2,128]{3,0,2,1:T(8,128)}, f32[512,1,2,128]{3,0,2,1:T(8,128)S(1)}, u32[]{:S(2)}) copy-start(f32[512,1,2,128]{3,0,2,1:T(8,128)S(1)} %get-tuple-element.588) | copy-start | bytes 1572868
  259.5 11.0 %copy-start.28 = (bf16[512,1,128]{2,0,1:T(8,128)(2,1)S(1)}, bf16[512,1,128]{2,0,1:T(8,128)(2,1)}, u32[]{:S(2)}) copy-start(bf16[512,1,128]{2,0,1:T(8,128)(2,1)} %param.63) | copy-start | bytes 393220
  263.6 15.0 %collective-permute-start.15 = (f32[1,512,1,256]{3,1,2,0:T(8,128)}, f32[1,512,1,256]{3,1,2,0:T(8,128)}, u32[]{:S(2)}, u32[]{:S(2)}) collective-permute-start(f32[1,512,1,256]{3,1,2,0:T(8,128)} %fusion.462), channel_id=1, source_target_pairs={{8,0},{16,8},{24,16},{32,24},{40,32},{48,40},{56,48},{64,56},{72,6... | collective-permute-start | bytes 1572872 | tf_op jit(solution)/shard_map/ppermute | solution.py:18
  275.0 5.6 %copy-start.1 = (bf16[256,4608]{1,0:T(8,128)(2,1)S(1)}, bf16[256,4608]{1,0:T(8,128)(2,1)}, u32[]{:S(2)}) copy-start(bf16[256,4608]{1,0:T(8,128)(2,1)} %param.64) | copy-start | bytes 7077892
  (12 other events, 18.7 us)
Sparse Core Ops, SparseCore 0:
  11.7 62.6 all-gather.1
  145.4 95.3 reduce-scatter.1
where the time goes:
time: 286 us; the launch traced here: 288 us
  matrix products  91.9 us (32%)
  waiting for transfers between devices  60.7 us (21%)
  starting transfers between devices  58.7 us (21%)
  other arithmetic  41.8 us (15%)
  between operations  20.6 us (7%)
  local copies, waits for them, and re-layouts  11.9 us (4%)
    ppermute x16, waiting for transfers between devices, passed_along(): return lax.ppermute(x, axis, pairs)  60.6 us
    ppermute x16, starting transfers between devices, passed_along(): return lax.ppermute(x, axis, pairs)  58.6 us
    dot_general x18, matrix products, block_scores(): jnp.einsum('tkgd,skd->kgts', grouped_q, key_block[..., :head_dim], prefer...  27.9 us
    dot_general x9, matrix products, forward_block(): jnp.einsum('kgts,skd->tkgd', probs_b, key_block[..., head_dim:], preferre...  27.8 us
    another operation x7, other arithmetic, per_device(): outgoing = jnp.stack(partials[anchor + distance:anchor + distance + amount])  14.4 us
    dot_general x9, matrix products, backward_block(): jnp.einsum('kgts,skd->tkgd', d_scores, key_block[..., :head_dim], preferr...  11.3 us
    cond x9, local copies, waits for them, and re-layouts, per_device(): lax.cond(jnp.any(masks[behind]), gradient_step, lambda: (zero_query, zero...  8.31 us
    dot_general x9, matrix products, backward_block(): jnp.einsum('tkgd,skd->kgts', d_grouped, key_block[..., head_dim:], prefer...  6.49 us
  transfers between devices with their start and end apart: 18, of which 14 were waited for; matrix products, arithmetic and copies ran while one was open for 47% of the time, Pallas kernels for 0%

commit v1 on v0

v1 whole, which is shorter than its diff:
```python
import functools
import math

import jax
import jax.numpy as jnp
from jax import lax
from jax.experimental import pallas as pl
from jax.experimental.pallas import tpu as pltpu
from jax.sharding import PartitionSpec as P

WINDOW = 4096
SIDE = 4
RING = 8
BACK = 8
SCALE = 1.0 / 12.0
EXP2_SCALE = SCALE * math.log2(math.e)
MASKED = -1e30
BF = jnp.bfloat16
F32 = jnp.float32
MESH = pl.DeviceIdType.MESH
NN = (((1,), (0,)), ((), ()))
NT = (((1,), (1,)), ((), ()))
TN = (((0,), (0,)), ((), ()))


def dot(a, b, dims):
    return lax.dot_general(a, b, dims, preferred_element_type=F32)


def kernel(
    lens, adv, q_ref, k_ref, v_ref, w_hbm, cot_ref,
    att_o, dq_o, dk_o, dv_o, dwo_o,
    sc, w, kv, q2, qT, lo, S, Pb, mx, rl, O2, att2,
    dA, dAs, dAsT, delta, dq, dS,
    dwf, psend, precv, ysend, yrecv, xsend, xrecv, xown,
    ssend, srecv, rsend, rrecv, lsend, lrecv,
    gs_sem, gr_sem, w_sem, hx_sem, hy_sem, hs_sem,
    pp_sem, yy_sem, xs_sem, xr_sem, ss_sem, rr_sem, ll_sem,
):
    s = lax.axis_index("seq")
    z = lax.axis_index("tp")
    core = lax.rem(s, 2)
    chip = s // 2
    y = lax.rem(chip, SIDE)
    x = chip // SIDE
    rows, fs = sc.shape[1], sc.shape[2]
    ebuf = S.at[:, : 2 * k_ref.shape[1], :]
    slices = sc.shape[0]
    part = rows // RING
    hd = k_ref.shape[1]
    own_rows = dwo_o.shape[0]

    def row_dev(i):
        return {"seq": x * (2 * SIDE) + lax.rem(y + i + SIDE, SIDE) * 2 + core}

    def col_dev(i):
        return {"seq": lax.rem(x + i + SIDE, SIDE) * (2 * SIDE) + y * 2 + core}

    def ring_dev(i):
        return {"tp": lax.rem(z + i + RING, RING)}

    sib_dev = {"seq": s + 1 - 2 * core}

    def remote(src, dst, send, recv, dev):
        return pltpu.make_async_remote_copy(
            src_ref=src, dst_ref=dst, send_sem=send, recv_sem=recv, device_id=dev, device_id_type=MESH
        )

    barrier = pltpu.get_barrier_semaphore()
    for dev in [sib_dev, ring_dev(1), ring_dev(-1)] + [f(i) for f in (row_dev, col_dev) for i in (1, 2, 3)]:
        pl.semaphore_signal(barrier, inc=1, device_id=dev, device_id_type=MESH)
    w_copy = pltpu.make_async_copy(w_hbm, w, w_sem)
    w_copy.start()

    place = s * rows + z * part + lax.broadcasted_iota(jnp.int32, (part, hd), 0)
    factor = jnp.full((part, hd), adv[0], F32)
    cum = jnp.int32(0)
    for r in range(lens.shape[0] - 1):
        cum = cum + lens[r]
        factor = jnp.where(place >= cum, adv[r + 1], factor)
    wide = jnp.concatenate([factor] * (fs // hd), axis=1)
    my_rows = pl.ds(pl.multiple_of(z * part, part), part)
    for f in range(slices):
        piece = cot_ref[:, f * fs : (f + 1) * fs].astype(F32)
        sc[f, my_rows, :] = (wide * piece).astype(BF)
    kv[0, :, :hd] = k_ref[...]
    kv[0, :, hd:] = v_ref[...]

    pl.semaphore_wait(barrier, 9)

    def chunk_rows(sign, away, kind):
        chunk = lax.rem(z - sign * away + RING, RING)
        half = part // 2
        if kind < 3:
            return pl.ds(pl.multiple_of(chunk * part, part), part)
        return pl.ds(pl.multiple_of(chunk * part + (0 if sign > 0 else half), half), half)

    def ring_copy(way, kind, f, away):
        sign = 1 - 2 * way
        ref = sc.at[f, chunk_rows(sign, away, kind)]
        return remote(ref, ref, gs_sem.at[way, kind, f], gr_sem.at[way, kind, f], ring_dev(sign))

    def arrived(kind, f):
        for way in (0, 1):
            ring_copy(way, kind, f, kind + 1).wait_recv()

    def event(kind, f):
        if kind:
            arrived(kind - 1, f)
        for way in (0, 1):
            ring_copy(way, kind, f, kind).start()

    event(0, 0)
    event(0, 1)

    hx = remote(kv.at[0], kv.at[8], hx_sem.at[0], hx_sem.at[1], col_dev(1))
    hx.start()

    def hy(i, slot):
        return remote(kv.at[slot], kv.at[2 * i], hy_sem.at[0, i], hy_sem.at[1, i], row_dev(i))

    def hs(j):
        return remote(
            kv.at[2 * (j - 1 + core)], kv.at[2 * j - 1], hs_sem.at[0, j], hs_sem.at[1, j], sib_dev
        )

    for i in (1, 2, 3):
        @pl.when(y + i < SIDE)
        def _():
            hy(i, 0).start()

    @pl.when(core == 0)
    def _():
        hs(1).start()

    q2[:rows, :] = q_ref[:, 0, :]
    q2[rows:, :] = q_ref[:, 1, :]
    qT[...] = q2[...].astype(F32).T.astype(BF)
    place = s * rows + lax.broadcasted_iota(jnp.int32, (rows, hd), 0)
    first = jnp.zeros((rows, hd), jnp.int32)
    cum = jnp.int32(0)
    for r in range(lens.shape[0] - 1):
        cum = cum + lens[r]
        first = jnp.where(place >= cum, cum, first)
    lo[...] = jnp.maximum(first, place - (WINDOW - 1)) - s * rows

    tile = 256
    tiles = 2 * rows // tile
    per_head = rows // tile

    def tile_rows(r):
        return pl.ds(pl.multiple_of(r * tile, tile), tile)

    def scores(d):
        def step(r, carry):
            at = tile_rows(r)
            raw = dot(q2[at, :], kv[d, :, :hd], NT)
            t0 = lax.rem(r, per_head) * tile
            low = lo[pl.ds(pl.multiple_of(t0, tile), tile), :] + d * rows
            best = None
            for c in range(rows // hd):
                col = lax.broadcasted_iota(jnp.int32, (tile, hd), 1) + c * hd
                seen = col >= low
                if d == 0:
                    seen = seen & (col <= lax.broadcasted_iota(jnp.int32, (tile, hd), 0) + t0)
                val = jnp.where(seen, raw[:, c * hd : (c + 1) * hd], MASKED)
                S[d, at, c * hd : (c + 1) * hd] = val
                best = val if best is None else jnp.maximum(best, val)
            mx[at, :] = best if d == 0 else jnp.maximum(mx[at, :], best)
            return carry

        lax.fori_loop(0, tiles, step, 0)

    def weigh(r):
        at = pl.ds(r * tile, tile)
        top = jnp.broadcast_to(jnp.max(mx[at, :], axis=1, keepdims=True), (tile, hd))
        mx[at, :] = top
        rl[at, :] = jnp.zeros((tile, hd), F32)
        O2[at, :] = jnp.zeros((tile, hd), F32)

        def step(d, carry):
            top = mx[at, :]
            total = rl[at, :]
            for c in range(rows // hd):
                p = jnp.exp2((S[d, at, c * hd : (c + 1) * hd] - top) * EXP2_SCALE)
                total = total + p
                Pb[d, at, c * hd : (c + 1) * hd] = p.astype(BF)
            rl[at, :] = total
            O2[at, :] += dot(Pb[d, at, :], kv[d, :, hd:], NN)
            return carry

        lax.fori_loop(0, BACK + 1, step, 0)
        inv = 1.0 / jnp.broadcast_to(jnp.sum(rl[at, :], axis=1, keepdims=True), (tile, hd))
        rl[at, :] = inv
        out = (O2[at, :] * inv).astype(BF)
        att2[at, :] = out
        t0, h = (r % per_head) * tile, r // per_head
        att_o[t0 : t0 + tile, h * hd : (h + 1) * hd] = out

    def project(f):
        term = dot(sc[f], w[:, f * fs : (f + 1) * fs], NT)
        if f == 0:
            dA[...] = term
        else:
            dA[...] += term

    def pair_copy(f):
        return remote(psend.at[f], precv.at[f], pp_sem.at[0, f], pp_sem.at[1, f], sib_dev)

    def weight_grad(f):
        def step(i, carry):
            at = pl.ds(pl.multiple_of(i * hd, hd), hd)
            dwf[f, at, :] = dot(sc[f, :, at], att_o[...], TN)
            return carry

        for i in range(fs // hd):
            step(i, 0)
        for j in range(SIDE):
            theirs = pl.ds(pl.multiple_of((2 * j + 1 - core) * own_rows, own_rows), own_rows)
            psend[f, j] = dwf[f, theirs, :].astype(BF)
        pair_copy(f).start()

    def pair_sum(f, j):
        mine = pl.ds(pl.multiple_of((2 * j + core) * own_rows, own_rows), own_rows)
        return dwf[f, mine, :] + precv[f, j].astype(F32)

    def row_copy(f, i):
        return remote(ysend.at[f, i], yrecv.at[f, i], yy_sem.at[0, f, i], yy_sem.at[1, f, i], row_dev(i))

    def row_send(f):
        pair_copy(f).wait_recv()
        for i in (1, 2, 3):
            ysend[f, i] = pair_sum(f, lax.rem(y + i, SIDE)).astype(BF)
            row_copy(f, i).start()

    def col_copy(f):
        slot = lax.rem(x - f + SIDE, SIDE)
        return remote(
            xsend.at[f], xrecv.at[slot], xs_sem.at[f], xr_sem.at[slot],
            {"seq": f * (2 * SIDE) + y * 2 + core},
        )

    def col_send(f):
        total = pair_sum(f, y)
        for i in (1, 2, 3):
            row_copy(f, i).wait_recv()
            total = total + yrecv[f, i].astype(F32)

        @pl.when(x == f)
        def _():
            xown[...] = total

        @pl.when(x != f)
        def _():
            xsend[f] = total.astype(BF)
            col_copy(f).start()

    def backward(d, out):
        for r in range(tiles):
            at = pl.ds(r * tile, tile)
            raw = dot(dAs[at, :], kv[d, :, hd:], NT)
            low = delta[at, :]
            for c in range(rows // hd):
                cs = slice(c * hd, (c + 1) * hd)
                dS[at, cs] = (Pb[d, at, cs].astype(F32) * (raw[:, cs] - low)).astype(BF)
            term = dot(dS[at, :], kv[d, :, :hd], NN)
            if d == BACK - 1:
                dq[at, :] = term
            else:
                dq[at, :] += term
        out[:hd, :] = dot(qT[...], dS[...], NN).astype(out.dtype)
        out[hd:, :] = dot(dAsT[...], Pb[d], NN).astype(out.dtype)

    def sib_copy(i):
        return remote(ssend.at[i], srecv.at[i], ss_sem.at[0, i], ss_sem.at[1, i], sib_dev)

    def back_copy(i):
        return remote(rsend.at[i], rrecv.at[i], rr_sem.at[0, i], rr_sem.at[1, i], row_dev(-i))

    relay = remote(lsend, lrecv, ll_sem.at[0], ll_sem.at[1], col_dev(-1))

    def odd(i):
        backward(2 * i - 1, ssend.at[i])
        sib_copy(i).start()

    def send_back(i):
        rsend[i] = (ebuf[i] + srecv[i + 1 - core].astype(F32)).astype(BF)
        back_copy(i).start()

    scores(0)
    event(1, 0)
    event(0, 2)
    hx.wait_recv()
    for i in (1, 2, 3):
        @pl.when(y + i >= SIDE)
        def _():
            hy(i, 8).start()
    scores(8)
    w_copy.wait()
    event(2, 0)
    event(1, 1)
    for j in (1, 2, 3, 4):
        if j < 4:
            hy(j, 0).wait_recv()
        if j == 1:
            @pl.when(core == 1)
            def _():
                hs(1).start()
        else:
            hs(j).start()
        if j < 4:
            scores(2 * j)
        hs(j).wait_recv()
        scores(2 * j - 1)
        if j == 3:
            event(3, 0)
    weigh(0)
    event(2, 1)
    event(0, 3)
    weigh(1)
    weigh(2)
    event(1, 2)
    weigh(3)
    event(3, 1)
    arrived(3, 0)
    project(0)
    weight_grad(0)
    event(2, 2)
    event(1, 3)
    arrived(3, 1)
    project(1)
    weight_grad(1)
    row_send(0)
    event(3, 2)
    event(2, 3)
    col_send(0)
    row_send(1)
    arrived(3, 2)
    project(2)
    weight_grad(2)
    event(3, 3)
    col_send(1)
    row_send(2)
    arrived(3, 3)
    project(3)

    for h in range(2):
        hr = slice(h * rows, (h + 1) * rows)
        rounded = dA[:, h * hd : (h + 1) * hd].astype(BF).astype(F32)
        scaled = (rounded * rl[hr, :]).astype(BF)
        dAs[hr, :] = scaled
        wide = scaled.astype(F32)
        dAsT[:, hr] = wide.T.astype(BF)
        d = jnp.sum(wide * att2[hr, :].astype(F32), axis=1, keepdims=True)
        delta[hr, :] = jnp.broadcast_to(d, (rows, hd))

    odd(4)
    weight_grad(3)
    odd(3)
    backward(6, ebuf.at[3])
    col_send(2)
    sib_copy(4).wait_recv()
    sib_copy(3).wait_recv()
    send_back(3)
    odd(2)
    row_send(3)
    backward(4, ebuf.at[2])
    sib_copy(2).wait_recv()
    send_back(2)
    odd(1)
    backward(2, ebuf.at[1])
    sib_copy(1).wait_recv()
    send_back(1)
    col_send(3)
    backward(8, ebuf.at[4])
    total = ebuf[4] + jnp.where(core == 1, srecv[4].astype(F32), 0.0)
    for i in (3, 2, 1):
        back_copy(i).wait_recv()
        total = total + jnp.where(y + i >= SIDE, rrecv[i].astype(F32), 0.0)
    lsend[...] = total.astype(BF)
    relay.start()
    backward(0, ebuf.at[0])
    for h in range(2):
        hr = slice(h * rows, (h + 1) * rows)
        dq_o[:, h * hd : (h + 1) * hd] = (dq[hr, :] * SCALE).astype(BF)
    own = xown[...]
    for i in (1, 2, 3):
        remote(xsend.at[i], xrecv.at[i], xs_sem.at[i], xr_sem.at[i], col_dev(i)).wait_recv()
        own = own + xrecv[i].astype(F32)
    dwo_o[...] = own
    total = ebuf[0] + jnp.where(core == 0, srecv[1].astype(F32), 0.0)
    for i in (1, 2, 3):
        total = total + jnp.where(y + i < SIDE, rrecv[i].astype(F32), 0.0)
    relay.wait_recv()
    total = total + lrecv[...].astype(F32)
    dk_o[...] = (total[:hd, :].T * SCALE).astype(BF)
    dv_o[...] = total[hd:, :].T.astype(BF)

    for f in range(slices):
        for way in (0, 1):
            for kind in range(4):
                ring_copy(way, kind, f, kind).wait_send()
        pair_copy(f).wait_send()
        for i in (1, 2, 3):
            row_copy(f, i).wait_send()

        @pl.when(x != f)
        def _():
            col_copy(f).wait_send()
    hx.wait_send()
    for i in (1, 2, 3):
        hy(i, 0).wait_send()
        back_copy(i).wait_send()
    for i in (1, 2, 3, 4):
        hs(i).wait_send()
        sib_copy(i).wait_send()
    relay.wait_send()


def per_device(queries, keys, values, out_weight, cotangent, advantages, lengths):
    rows, heads, hd = queries.shape
    width = heads * hd
    depth = cotangent.shape[1]
    slices = SIDE
    fs = depth // slices
    own = depth // lax.axis_size("seq")
    q_rows = heads * rows
    vmem = pl.BlockSpec(memory_space=pltpu.VMEM)
    smem = pl.BlockSpec(memory_space=pltpu.SMEM)
    dma = pltpu.SemaphoreType.DMA
    V = pltpu.VMEM
    out = pl.pallas_call(
        kernel,
        out_shape=[
            jax.ShapeDtypeStruct((rows, width), BF),
            jax.ShapeDtypeStruct((rows, width), BF),
            jax.ShapeDtypeStruct((rows, hd), BF),
            jax.ShapeDtypeStruct((rows, hd), BF),
            jax.ShapeDtypeStruct((own, width), F32),
        ],
        in_specs=[smem, smem, vmem, vmem, vmem, pl.BlockSpec(memory_space=pl.ANY), vmem],
        out_specs=[vmem] * 5,
        scratch_shapes=[
            V((slices, rows, fs), BF),
            V((width, depth), BF),
            V((BACK + 1, rows, 2 * hd), BF),
            V((q_rows, hd), BF),
            V((hd, q_rows), BF),
            V((rows, hd), jnp.int32),
            V((BACK + 1, q_rows, rows), F32),
            V((BACK + 1, q_rows, rows), BF),
            V((q_rows, hd), F32),
            V((q_rows, hd), F32),
            V((q_rows, hd), F32),
            V((q_rows, hd), BF),
            V((rows, width), F32),
            V((q_rows, hd), BF),
            V((hd, q_rows), BF),
            V((q_rows, hd), F32),
            V((q_rows, hd), F32),
            V((q_rows, rows), BF),
            V((slices, fs, width), F32),
            V((slices, SIDE, own, width), BF),
            V((slices, SIDE, own, width), BF),
            V((slices, SIDE, own, width), BF),
            V((slices, SIDE, own, width), BF),
            V((slices, own, width), BF),
            V((SIDE, own, width), BF),
            V((own, width), F32),
            V((5, 2 * hd, rows), BF),
            V((5, 2 * hd, rows), BF),
            V((4, 2 * hd, rows), BF),
            V((4, 2 * hd, rows), BF),
            V((2 * hd, rows), BF),
            V((2 * hd, rows), BF),
            dma((2, 4, slices)),
            dma((2, 4, slices)),
            dma,
            dma((2,)),
            dma((2, 4)),
            dma((2, 5)),
            dma((2, slices)),
            dma((2, slices, 4)),
            dma((slices,)),
            dma((4,)),
            dma((2, 5)),
            dma((2, 4)),
            dma((2,)),
        ],
        compiler_params=pltpu.CompilerParams(
            collective_id=0, has_side_effects=True, vmem_limit_bytes=60 * 1024 * 1024
        ),
        cost_estimate=pl.CostEstimate(flops=9 * 10**9, bytes_accessed=5 * 10**6, transcendentals=5 * 10**6),
        name="rollout_attention",
    )(lengths, advantages, queries, keys.reshape(rows, hd), values.reshape(rows, hd), out_weight, cotangent)
    attention, d_queries, d_keys, d_values, d_weight = out
    return (
        attention.reshape(rows, heads, hd),
        d_queries.reshape(rows, heads, hd),
        d_keys.reshape(rows, 1, hd),
        d_values.reshape(rows, 1, hd),
        d_weight,
    )


def solution(mesh):
    tokens = P("seq", "tp", None)
    return jax.shard_map(
        per_device,
        mesh=mesh,
        in_specs=(tokens, tokens, tokens, P("tp", None), P(("seq", "tp"), None), P(), P()),
        out_specs=(tokens, tokens, tokens, tokens, P("seq", "tp")),
        check_vma=False,
    )
```

time: 286 us -> 111 us (0.39)
  the two profiles are of different devices: /device:TPU:4 before, /device:TPU:22 now
where the time goes in v1:
time: 111 us
  Pallas kernels  102 us (92%)
  local copies, waits for them, and re-layouts  8.15 us (7%)
    pallas_call x1, Pallas kernels, per_device(): pl.pallas_call(kernel, out_shape=[jax.ShapeDtypeStruct((rows, width), BF)...  102 us
    unnamed x3, local copies, waits for them, and re-layouts  4.71 us

profile of v1, /device:TPU:22, one launch (start us, length us, event | category | flops | bytes accessed | tf_op | source)
XLA Modules:
  0.0 111.1 jit_solution(337514663163472649)
XLA Ops:
  0.6 102.3 %rollout_attention.1 = (bf16[512,256]{1,0:T(8,128)(2,1)}, bf16[512,256]{1,0:T(8,128)(2,1)}, bf16[512,128]{1,0:T(8,128)(2,1)}, bf16[512,128]{1,0:T(8,128)(2,1)}, f32[144,256]{1,0:T(8,128)}) custom-call(s32[8]{0:T(128)} %lens.1, f32[8]{0:T(128)} %adv.1, bf16[512,2,128]{2,1,0:T(2,128)(2,1)} %q_ref.1, bf16[512,128]{1,0:T(8,128)(2,1)} %bitcast.6, ...), custom_call_target="tpu_custom_call" | custom-call | flops 8999999488 | bytes 5000000 | tf_op jit(solution)/shard_map/rollout_attention/pallas_call | solution.py:432
  103.0 1.7 %reshape.30 = bf16[512,2,128]{2,1,0:T(2,128)(2,1)} reshape(bf16[512,256]{1,0:T(8,128)(2,1)} %get-tuple-element.10) | data formatting | bytes 524288 | tf_op jit(solution)/shard_map/reshape | solution.py:498
  104.7 1.7 %reshape.31 = bf16[512,2,128]{2,1,0:T(2,128)(2,1)} reshape(bf16[512,256]{1,0:T(8,128)(2,1)} %get-tuple-element.11) | data formatting | bytes 524288 | tf_op jit(solution)/shard_map/reshape | solution.py:499
  106.4 1.6 %copy.15 = bf16[512,1,128]{2,0,1:T(8,128)(2,1)} copy(bf16[512,1,128]{2,0,1:T(8,128)(2,1)} %bitcast.5) | data formatting | bytes 262144
  108.0 1.6 %copy.16 = bf16[512,1,128]{2,0,1:T(8,128)(2,1)} copy(bf16[512,1,128]{2,0,1:T(8,128)(2,1)} %bitcast.4) | data formatting | bytes 262144
  109.6 1.6 %copy.17 = f32[144,256]{1,0:T(8,128)} copy(f32[144,256]{1,0:T(8,128)} %get-tuple-element.24) | data formatting | bytes 294912

commit v2 on v1

--- a/solution.py
+++ b/solution.py
@@ -32,7 +32,7 @@
     att_o, dq_o, dk_o, dv_o, dwo_o,
     sc, w, kv, q2, qT, lo, S, Pb, mx, rl, O2, att2,
     dA, dAs, dAsT, delta, dq, dS,
-    dwf, psend, precv, ysend, yrecv, xsend, xrecv, xown,
+    psend, precv, ysend, yrecv, yown, xsend, xrecv, xown,
     ssend, srecv, rsend, rrecv, lsend, lrecv,
     gs_sem, gr_sem, w_sem, hx_sem, hy_sem, hs_sem,
     pp_sem, yy_sem, xs_sem, xr_sem, ss_sem, rr_sem, ll_sem,
@@ -67,7 +67,10 @@
         )
 
     barrier = pltpu.get_barrier_semaphore()
-    for dev in [sib_dev, ring_dev(1), ring_dev(-1)] + [f(i) for f in (row_dev, col_dev) for i in (1, 2, 3)]:
+    next_dev = {"seq": lax.rem(s + 2, 2 * SIDE * SIDE)}
+    last_dev = {"seq": lax.rem(s - 2 + 2 * SIDE * SIDE, 2 * SIDE * SIDE)}
+    around = [f(i) for f in (row_dev, col_dev) for i in (1, 2, 3)]
+    for dev in [sib_dev, ring_dev(1), ring_dev(-1), next_dev] + around:
         pl.semaphore_signal(barrier, inc=1, device_id=dev, device_id_type=MESH)
     w_copy = pltpu.make_async_copy(w_hbm, w, w_sem)
     w_copy.start()
@@ -86,7 +89,7 @@
     kv[0, :, :hd] = k_ref[...]
     kv[0, :, hd:] = v_ref[...]
 
-    pl.semaphore_wait(barrier, 9)
+    pl.semaphore_wait(barrier, 10)
 
     def chunk_rows(sign, away, kind):
         chunk = lax.rem(z - sign * away + RING, RING)
@@ -113,16 +116,20 @@
     event(0, 0)
     event(0, 1)
 
-    hx = remote(kv.at[0], kv.at[8], hx_sem.at[0], hx_sem.at[1], col_dev(1))
-    hx.start()
+    def hx():
+        return remote(kv.at[0], kv.at[8], hx_sem.at[0], hx_sem.at[1], col_dev(1))
+
+    hx().start()
 
     def hy(i, slot):
         return remote(kv.at[slot], kv.at[2 * i], hy_sem.at[0, i], hy_sem.at[1, i], row_dev(i))
 
-    def hs(j):
-        return remote(
-            kv.at[2 * (j - 1 + core)], kv.at[2 * j - 1], hs_sem.at[0, j], hs_sem.at[1, j], sib_dev
-        )
+    def hs(i):
+        j = i + 1 - core
+        return remote(kv.at[2 * i], kv.at[2 * j - 1], hs_sem.at[0, j], hs_sem.at[1, j], sib_dev)
+
+    def hs_from(j):
+        return remote(kv.at[2 * j], kv.at[2 * j - 1], hs_sem.at[0, j], hs_sem.at[1, j], sib_dev)
 
     for i in (1, 2, 3):
         @pl.when(y + i < SIDE)
@@ -131,7 +138,7 @@
 
     @pl.when(core == 0)
     def _():
-        hs(1).start()
+        hs(0).start()
 
     q2[:rows, :] = q_ref[:, 0, :]
     q2[rows:, :] = q_ref[:, 1, :]
@@ -171,12 +178,12 @@
 
         lax.fori_loop(0, tiles, step, 0)
 
-    def weigh(r):
+    def weigh(r, last):
         at = pl.ds(r * tile, tile)
-        top = jnp.broadcast_to(jnp.max(mx[at, :], axis=1, keepdims=True), (tile, hd))
-        mx[at, :] = top
-        rl[at, :] = jnp.zeros((tile, hd), F32)
-        O2[at, :] = jnp.zeros((tile, hd), F32)
+        if not last:
+            mx[at, :] = jnp.broadcast_to(jnp.max(mx[at, :], axis=1, keepdims=True), (tile, hd))
+            rl[at, :] = jnp.zeros((tile, hd), F32)
+            O2[at, :] = jnp.zeros((tile, hd), F32)
 
         def step(d, carry):
             top = mx[at, :]
@@ -189,7 +196,11 @@
             O2[at, :] += dot(Pb[d, at, :], kv[d, :, hd:], NN)
             return carry
 
-        lax.fori_loop(0, BACK + 1, step, 0)
+        middle = BACK // 2
+        if not last:
+            lax.fori_loop(0, middle, step, 0)
+            return
+        lax.fori_loop(middle, BACK + 1, step, 0)
         inv = 1.0 / jnp.broadcast_to(jnp.sum(rl[at, :], axis=1, keepdims=True), (tile, hd))
         rl[at, :] = inv
         out = (O2[at, :] * inv).astype(BF)
@@ -207,30 +218,40 @@
     def pair_copy(f):
         return remote(psend.at[f], precv.at[f], pp_sem.at[0, f], pp_sem.at[1, f], sib_dev)
 
+    def weight_rows(f, j, which):
+        width = att_o.shape[1]
+        at = pl.ds(pl.multiple_of((2 * (j % 2) + which) * own_rows, own_rows), own_rows)
+        return S[BACK - f, at, (j // 2) * width : (j // 2 + 1) * width]
+
     def weight_grad(f):
-        def step(i, carry):
-            at = pl.ds(pl.multiple_of(i * hd, hd), hd)
-            dwf[f, at, :] = dot(sc[f, :, at], att_o[...], TN)
-            return carry
-
+        width = att_o.shape[1]
+        cut = fs // 2
         for i in range(fs // hd):
-            step(i, 0)
+            term = dot(sc[f, :, i * hd : (i + 1) * hd], att_o[...], TN)
+            for side in (0, 1):
+                first, last = max(i * hd, side * cut), min((i + 1) * hd, (side + 1) * cut)
+                if first < last:
+                    S[BACK - f, first - side * cut : last - side * cut, pl.ds(side * width, width)] = (
+                        term[first - i * hd : last - i * hd]
+                    )
         for j in range(SIDE):
-            theirs = pl.ds(pl.multiple_of((2 * j + 1 - core) * own_rows, own_rows), own_rows)
-            psend[f, j] = dwf[f, theirs, :].astype(BF)
+            psend[f, j] = weight_rows(f, j, 1 - core).astype(BF)
         pair_copy(f).start()
-
-    def pair_sum(f, j):
-        mine = pl.ds(pl.multiple_of((2 * j + core) * own_rows, own_rows), own_rows)
-        return dwf[f, mine, :] + precv[f, j].astype(F32)
 
     def row_copy(f, i):
         return remote(ysend.at[f, i], yrecv.at[f, i], yy_sem.at[0, f, i], yy_sem.at[1, f, i], row_dev(i))
 
     def row_send(f):
         pair_copy(f).wait_recv()
+        for j in range(SIDE):
+            both = weight_rows(f, j, core) + precv[f, j].astype(F32)
+            ysend[f, lax.rem(j - y + SIDE, SIDE)] = both.astype(BF)
+
+            @pl.when(y == j)
+            def _():
+                yown[f] = both
+
         for i in (1, 2, 3):
-            ysend[f, i] = pair_sum(f, lax.rem(y + i, SIDE)).astype(BF)
             row_copy(f, i).start()
 
     def col_copy(f):
@@ -240,8 +261,11 @@
             {"seq": f * (2 * SIDE) + y * 2 + core},
         )
 
+    def col_from(i):
+        return remote(xsend.at[i], xrecv.at[i], xs_sem.at[i], xr_sem.at[i], col_dev(i))
+
     def col_send(f):
-        total = pair_sum(f, y)
+        total = yown[f]
         for i in (1, 2, 3):
             row_copy(f, i).wait_recv()
             total = total + yrecv[f, i].astype(F32)
@@ -255,7 +279,7 @@
             xsend[f] = total.astype(BF)
             col_copy(f).start()
 
-    def backward(d, out):
+    def backward(d, out, first=False):
         for r in range(tiles):
             at = pl.ds(r * tile, tile)
             raw = dot(dAs[at, :], kv[d, :, hd:], NT)
@@ -264,7 +288,7 @@
                 cs = slice(c * hd, (c + 1) * hd)
                 dS[at, cs] = (Pb[d, at, cs].astype(F32) * (raw[:, cs] - low)).astype(BF)
             term = dot(dS[at, :], kv[d, :, :hd], NN)
-            if d == BACK - 1:
+            if first:
                 dq[at, :] = term
             else:
                 dq[at, :] += term
@@ -274,73 +298,96 @@
     def sib_copy(i):
         return remote(ssend.at[i], srecv.at[i], ss_sem.at[0, i], ss_sem.at[1, i], sib_dev)
 
-    def back_copy(i):
-        return remote(rsend.at[i], rrecv.at[i], rr_sem.at[0, i], rr_sem.at[1, i], row_dev(-i))
-
-    relay = remote(lsend, lrecv, ll_sem.at[0], ll_sem.at[1], col_dev(-1))
-
-    def odd(i):
-        backward(2 * i - 1, ssend.at[i])
+    def half(ref, h):
+        return ref.at[pl.ds(h * hd, hd)]
+
+    def back_copy(i, h):
+        dev = last_dev if i == 1 else row_dev(-i)
+        return remote(half(rsend.at[i], h), half(rrecv.at[i], h), rr_sem.at[0, i, h], rr_sem.at[1, i, h], dev)
+
+    def relay(h):
+        return remote(half(lsend, h), half(lrecv, h), ll_sem.at[0, h], ll_sem.at[1, h], col_dev(-1))
+
+    def odd(i, first=False):
+        backward(2 * i - 1, ssend.at[i], first)
         sib_copy(i).start()
 
     def send_back(i):
-        rsend[i] = (ebuf[i] + srecv[i + 1 - core].astype(F32)).astype(BF)
-        back_copy(i).start()
+        j = i + 1 - core
+        sib_copy(j).wait_recv()
+        for h in (0, 1):
+            hs_ = pl.ds(h * hd, hd)
+            rsend[i, hs_, :] = (ebuf[i, hs_, :] + srecv[j, hs_, :].astype(F32)).astype(BF)
+            back_copy(i, h).start()
+
+    def relay_in():
+        hx().wait_recv()
+        for i in (1, 2, 3):
+            @pl.when(y + i >= SIDE)
+            def _():
+                hy(i, 8).start()
+
+        @pl.when(core == 1)
+        def _():
+            hs(4).start()
+
+    def even_in(i):
+        hy(i, 0).wait_recv()
+        hs(i).start()
+        scores(2 * i)
+
+    def odd_in(j):
+        hs_from(j).wait_recv()
+        scores(2 * j - 1)
 
     scores(0)
     event(1, 0)
     event(0, 2)
-    hx.wait_recv()
-    for i in (1, 2, 3):
-        @pl.when(y + i >= SIDE)
-        def _():
-            hy(i, 8).start()
+    relay_in()
     scores(8)
+    event(1, 1)
+    event(2, 0)
+    even_in(1)
+    event(2, 1)
+    event(1, 2)
+    odd_in(1)
+    even_in(3)
+    event(3, 0)
+    event(0, 3)
+    even_in(2)
+    odd_in(2)
+    odd_in(3)
+    event(3, 1)
+    odd_in(4)
+    weigh(0, False)
+    weigh(0, True)
+    event(2, 2)
+    weigh(1, False)
+    weigh(1, True)
     w_copy.wait()
-    event(2, 0)
-    event(1, 1)
-    for j in (1, 2, 3, 4):
-        if j < 4:
-            hy(j, 0).wait_recv()
-        if j == 1:
-            @pl.when(core == 1)
-            def _():
-                hs(1).start()
-        else:
-            hs(j).start()
-        if j < 4:
-            scores(2 * j)
-        hs(j).wait_recv()
-        scores(2 * j - 1)
-        if j == 3:
-            event(3, 0)
-    weigh(0)
-    event(2, 1)
-    event(0, 3)
-    weigh(1)
-    weigh(2)
-    event(1, 2)
-    weigh(3)
-    event(3, 1)
     arrived(3, 0)
     project(0)
-    weight_grad(0)
-    event(2, 2)
+    weigh(2, False)
+    weigh(2, True)
     event(1, 3)
+    weigh(3, False)
     arrived(3, 1)
     project(1)
+    weigh(3, True)
+    weight_grad(0)
+    event(3, 2)
+
     weight_grad(1)
     row_send(0)
-    event(3, 2)
     event(2, 3)
-    col_send(0)
     row_send(1)
     arrived(3, 2)
     project(2)
     weight_grad(2)
+    col_send(0)
     event(3, 3)
+    row_send(2)
     col_send(1)
-    row_send(2)
     arrived(3, 3)
     project(3)
 
@@ -354,47 +401,61 @@
         d = jnp.sum(wide * att2[hr, :].astype(F32), axis=1, keepdims=True)
         delta[hr, :] = jnp.broadcast_to(d, (rows, hd))
 
-    odd(4)
-    weight_grad(3)
+    odd(4, True)
     odd(3)
     backward(6, ebuf.at[3])
-    col_send(2)
-    sib_copy(4).wait_recv()
-    sib_copy(3).wait_recv()
     send_back(3)
+    weight_grad(3)
     odd(2)
-    row_send(3)
     backward(4, ebuf.at[2])
-    sib_copy(2).wait_recv()
     send_back(2)
     odd(1)
+    col_send(2)
+    row_send(3)
+    backward(8, ebuf.at[4])
     backward(2, ebuf.at[1])
-    sib_copy(1).wait_recv()
     send_back(1)
-    col_send(3)
-    backward(8, ebuf.at[4])
-    total = ebuf[4] + jnp.where(core == 1, srecv[4].astype(F32), 0.0)
-    for i in (3, 2, 1):
-        back_copy(i).wait_recv()
-        total = total + jnp.where(y + i >= SIDE, rrecv[i].astype(F32), 0.0)
-    lsend[...] = total.astype(BF)
-    relay.start()
     backward(0, ebuf.at[0])
     for h in range(2):
         hr = slice(h * rows, (h + 1) * rows)
         dq_o[:, h * hd : (h + 1) * hd] = (dq[hr, :] * SCALE).astype(BF)
+
+    @pl.when(core == 1)
+    def _():
+        sib_copy(4).wait_recv()
+
+    for h in (0, 1):
+        hr = pl.ds(h * hd, hd)
+        total = ebuf[4, hr, :] + jnp.where(core == 1, srecv[4, hr, :].astype(F32), 0.0)
+        for i in (3, 2):
+            back_copy(i, h).wait_recv()
+            total = total + jnp.where(y + i >= SIDE, rrecv[i, hr, :].astype(F32), 0.0)
+        lsend[hr, :] = total.astype(BF)
+        relay(h).start()
+    col_send(3)
     own = xown[...]
     for i in (1, 2, 3):
-        remote(xsend.at[i], xrecv.at[i], xs_sem.at[i], xr_sem.at[i], col_dev(i)).wait_recv()
+        col_from(i).wait_recv()
         own = own + xrecv[i].astype(F32)
     dwo_o[...] = own
-    total = ebuf[0] + jnp.where(core == 0, srecv[1].astype(F32), 0.0)
-    for i in (1, 2, 3):
-        total = total + jnp.where(y + i < SIDE, rrecv[i].astype(F32), 0.0)
-    relay.wait_recv()
-    total = total + lrecv[...].astype(F32)
-    dk_o[...] = (total[:hd, :].T * SCALE).astype(BF)
-    dv_o[...] = total[hd:, :].T.astype(BF)
+
+    @pl.when(core == 0)
+    def _():
+        sib_copy(1).wait_recv()
+
+    for h in (0, 1):
+        hr = pl.ds(h * hd, hd)
+        total = ebuf[0, hr, :] + jnp.where(core == 0, srecv[1, hr, :].astype(F32), 0.0)
+        for i in (3, 2):
+            total = total + jnp.where(y + i < SIDE, rrecv[i, hr, :].astype(F32), 0.0)
+        back_copy(1, h).wait_recv()
+        total = total + rrecv[1, hr, :].astype(F32)
+        relay(h).wait_recv()
+        total = total + lrecv[hr, :].astype(F32)
+        if h == 0:
+            dk_o[...] = (total.T * SCALE).astype(BF)
+        else:
+            dv_o[...] = total.T.astype(BF)
 
     for f in range(slices):
         for way in (0, 1):
@@ -407,14 +468,22 @@
         @pl.when(x != f)
         def _():
             col_copy(f).wait_send()
-    hx.wait_send()
+    hx().wait_send()
     for i in (1, 2, 3):
         hy(i, 0).wait_send()
-        back_copy(i).wait_send()
-    for i in (1, 2, 3, 4):
-        hs(i).wait_send()
-        sib_copy(i).wait_send()
-    relay.wait_send()
+        for h in (0, 1):
+            back_copy(i, h).wait_send()
+    for j in (1, 2, 3, 4):
+        hs_from(j).wait_send()
+        sib_copy(j).wait_send()
+    for h in (0, 1):
+        relay(h).wait_send()
+
+
+def finish(*refs):
+    count = len(refs) // 2
+    for given, laid in zip(refs[:count], refs[count:]):
+        laid[...] = given[...].reshape(laid.shape)
 
 
 def per_device(queries, keys, values, out_weight, cotangent, advantages, lengths):
@@ -426,6 +495,7 @@
     own = depth // lax.axis_size("seq")
     q_rows = heads * rows
     vmem = pl.BlockSpec(memory_space=pltpu.VMEM)
+    anywhere = pl.BlockSpec(memory_space=pl.ANY)
     smem = pl.BlockSpec(memory_space=pltpu.SMEM)
     dma = pltpu.SemaphoreType.DMA
     V = pltpu.VMEM
@@ -438,7 +508,7 @@
             jax.ShapeDtypeStruct((rows, hd), BF),
             jax.ShapeDtypeStruct((own, width), F32),
         ],
-        in_specs=[smem, smem, vmem, vmem, vmem, pl.BlockSpec(memory_space=pl.ANY), vmem],
+        in_specs=[smem, smem, vmem, vmem, vmem, anywhere, vmem],
         out_specs=[vmem] * 5,
         scratch_shapes=[
             V((slices, rows, fs), BF),
@@ -459,11 +529,11 @@
             V((q_rows, hd), F32),
             V((q_rows, hd), F32),
             V((q_rows, rows), BF),
-            V((slices, fs, width), F32),
             V((slices, SIDE, own, width), BF),
             V((slices, SIDE, own, width), BF),
             V((slices, SIDE, own, width), BF),
             V((slices, SIDE, own, width), BF),
+            V((slices, own, width), F32),
             V((slices, own, width), BF),
             V((SIDE, own, width), BF),
             V((own, width), F32),
@@ -484,8 +554,8 @@
             dma((slices,)),
             dma((4,)),
             dma((2, 5)),
-            dma((2, 4)),
-            dma((2,)),
+            dma((2, 4, 2)),
+            dma((2, 2)),
         ],
         compiler_params=pltpu.CompilerParams(
             collective_id=0, has_side_effects=True, vmem_limit_bytes=60 * 1024 * 1024
@@ -493,14 +563,20 @@
         cost_estimate=pl.CostEstimate(flops=9 * 10**9, bytes_accessed=5 * 10**6, transcendentals=5 * 10**6),
         name="rollout_attention",
     )(lengths, advantages, queries, keys.reshape(rows, hd), values.reshape(rows, hd), out_weight, cotangent)
-    attention, d_queries, d_keys, d_values, d_weight = out
-    return (
-        attention.reshape(rows, heads, hd),
-        d_queries.reshape(rows, heads, hd),
-        d_keys.reshape(rows, 1, hd),
-        d_values.reshape(rows, 1, hd),
-        d_weight,
-    )
+    attention, d_queries, d_keys, d_values, d_weight = pl.pallas_call(
+        finish,
+        out_shape=[
+            jax.ShapeDtypeStruct((rows, heads, hd), BF),
+            jax.ShapeDtypeStruct((rows, heads, hd), BF),
+            jax.ShapeDtypeStruct((rows, hd), BF),
+            jax.ShapeDtypeStruct((rows, hd), BF),
+            jax.ShapeDtypeStruct((own, width), F32),
+        ],
+        in_specs=[vmem] * 5,
+        out_specs=[vmem] * 5,
+        name="lay_out_results",
+    )(*out)
+    return (attention, d_queries, d_keys.reshape(rows, 1, hd), d_values.reshape(rows, 1, hd), d_weight)
 
 
 def solution(mesh):

time: 111 us -> 96.2 us (0.87)
  the two profiles are of different devices: /device:TPU:22 before, /device:TPU:6 now
where the time goes in v2:
time: 96.2 us; the launch traced here: 96 us
  Pallas kernels  95.4 us (99%)
    pallas_call x1, Pallas kernels, per_device(): pl.pallas_call(kernel, out_shape=[jax.ShapeDtypeStruct((rows, width), BF)...  93.3 us
    pallas_call x1, Pallas kernels, per_device(): pl.pallas_call(finish, out_shape=[jax.ShapeDtypeStruct((rows, heads, hd),...  2.12 us

profile of v2, /device:TPU:6, one launch (start us, length us, event | category | flops | bytes accessed | tf_op | source)
XLA Modules:
  0.0 96.0 jit_solution(8043698007945836716)
XLA Ops:
  0.6 93.3 %rollout_attention.1 = (bf16[512,256]{1,0:T(8,128)(2,1)}, bf16[512,256]{1,0:T(8,128)(2,1)}, bf16[512,128]{1,0:T(8,128)(2,1)}, bf16[512,128]{1,0:T(8,128)(2,1)}, f32[144,256]{1,0:T(8,128)}) custom-call(s32[8]{0:T(128)} %lens.1, f32[8]{0:T(128)} %adv.1, bf16[512,2,128]{2,1,0:T(2,128)(2,1)} %q_ref.1, bf16[512,128]{1,0:T(8,128)(2,1)} %bitcast.4, ...), custom_call_target="tpu_custom_call" | custom-call | flops 8999999488 | bytes 5000000 | tf_op jit(solution)/shard_map/rollout_attention/pallas_call | solution.py:502
  93.9 2.1 %lay_out_results.1 = (bf16[512,2,128]{2,1,0:T(2,128)(2,1)}, bf16[512,2,128]{2,1,0:T(2,128)(2,1)}, bf16[512,128]{1,0:T(8,128)(2,1)}, bf16[512,128]{1,0:T(8,128)(2,1)}, f32[144,256]{1,0:T(8,128)}) custom-call(bf16[512,256]{1,0:T(8,128)(2,1)} %get-tuple-element.15.refs_0_, bf16[512,256]{1,0:T(8,128)(2,1)} %get-tuple-element.16.refs_1_, ...), custom_call_target="tpu_custom_call" | custom-call | tf_op jit(solution)/shard_map/lay_out_results/pallas_call | solution.py:566

commit v3 on v2

--- a/solution.py
+++ b/solution.py
@@ -30,7 +30,7 @@
 def kernel(
     lens, adv, q_ref, k_ref, v_ref, w_hbm, cot_ref,
     att_o, dq_o, dk_o, dv_o, dwo_o,
-    sc, w, kv, q2, qT, lo, S, Pb, mx, rl, O2, att2,
+    att, sc, w, kv, q2, qT, lo, hi, S, Pb, mx, rl, O2, att2,
     dA, dAs, dAsT, delta, dq, dS,
     psend, precv, ysend, yrecv, yown, xsend, xrecv, xown,
     ssend, srecv, rsend, rrecv, lsend, lrecv,
@@ -44,7 +44,7 @@
     y = lax.rem(chip, SIDE)
     x = chip // SIDE
     rows, fs = sc.shape[1], sc.shape[2]
-    ebuf = S.at[:, : 2 * k_ref.shape[1], :]
+    ebuf = S.at[:, pl.ds(fs // 2, 2 * k_ref.shape[1]), :]
     slices = sc.shape[0]
     part = rows // RING
     hd = k_ref.shape[1]
@@ -82,7 +82,7 @@
         cum = cum + lens[r]
         factor = jnp.where(place >= cum, adv[r + 1], factor)
     wide = jnp.concatenate([factor] * (fs // hd), axis=1)
-    my_rows = pl.ds(pl.multiple_of(z * part, part), part)
+    my_rows = pl.ds(0, part)
     for f in range(slices):
         piece = cot_ref[:, f * fs : (f + 1) * fs].astype(F32)
         sc[f, my_rows, :] = (wide * piece).astype(BF)
@@ -91,27 +91,32 @@
 
     pl.semaphore_wait(barrier, 10)
 
-    def chunk_rows(sign, away, kind):
-        chunk = lax.rem(z - sign * away + RING, RING)
-        half = part // 2
+    offsets = (0, 1, -1, 2, -2, 3, -3, 4)
+
+    def chunk_of(p):
+        return pl.ds(pl.multiple_of(lax.rem(z + offsets[p] + RING, RING) * part, part), part)
+
+    def spot(away, kind, way):
+        p = offsets.index(away if abs(away) < 4 else 4)
         if kind < 3:
-            return pl.ds(pl.multiple_of(chunk * part, part), part)
-        return pl.ds(pl.multiple_of(chunk * part + (0 if sign > 0 else half), half), half)
-
-    def ring_copy(way, kind, f, away):
+            return pl.ds(p * part, part)
+        return pl.ds(p * part + way * (part // 2), part // 2)
+
+    def ring_copy(way, kind, f):
         sign = 1 - 2 * way
-        ref = sc.at[f, chunk_rows(sign, away, kind)]
-        return remote(ref, ref, gs_sem.at[way, kind, f], gr_sem.at[way, kind, f], ring_dev(sign))
+        src = sc.at[f, spot(-sign * kind, kind, way)]
+        dst = sc.at[f, spot(-sign * (kind + 1), kind, way)]
+        return remote(src, dst, gs_sem.at[way, kind, f], gr_sem.at[way, kind, f], ring_dev(sign))
 
     def arrived(kind, f):
         for way in (0, 1):
-            ring_copy(way, kind, f, kind + 1).wait_recv()
+            ring_copy(way, kind, f).wait_recv()
 
     def event(kind, f):
         if kind:
             arrived(kind - 1, f)
         for way in (0, 1):
-            ring_copy(way, kind, f, kind).start()
+            ring_copy(way, kind, f).start()
 
     event(0, 0)
     event(0, 1)
@@ -140,16 +145,20 @@
     def _():
         hs(0).start()
 
-    q2[:rows, :] = q_ref[:, 0, :]
-    q2[rows:, :] = q_ref[:, 1, :]
+    for p in range(RING):
+        here = pl.ds(p * part, part)
+        for h in range(2):
+            q2[h * rows + p * part : h * rows + (p + 1) * part, :] = q_ref[chunk_of(p), h, :]
+        local = lax.rem(z + offsets[p] + RING, RING) * part + lax.broadcasted_iota(jnp.int32, (part, hd), 0)
+        place = s * rows + local
+        first = jnp.zeros((part, hd), jnp.int32)
+        cum = jnp.int32(0)
+        for r in range(lens.shape[0] - 1):
+            cum = cum + lens[r]
+            first = jnp.where(place >= cum, cum, first)
+        lo[here, :] = jnp.maximum(first, place - (WINDOW - 1)) - s * rows
+        hi[here, :] = local
     qT[...] = q2[...].astype(F32).T.astype(BF)
-    place = s * rows + lax.broadcasted_iota(jnp.int32, (rows, hd), 0)
-    first = jnp.zeros((rows, hd), jnp.int32)
-    cum = jnp.int32(0)
-    for r in range(lens.shape[0] - 1):
-        cum = cum + lens[r]
-        first = jnp.where(place >= cum, cum, first)
-    lo[...] = jnp.maximum(first, place - (WINDOW - 1)) - s * rows
 
     tile = 256
     tiles = 2 * rows // tile
@@ -169,7 +178,7 @@
                 col = lax.broadcasted_iota(jnp.int32, (tile, hd), 1) + c * hd
                 seen = col >= low
                 if d == 0:
-                    seen = seen & (col <= lax.broadcasted_iota(jnp.int32, (tile, hd), 0) + t0)
+                    seen = seen & (col <= hi[pl.ds(pl.multiple_of(t0, tile), tile), :])
                 val = jnp.where(seen, raw[:, c * hd : (c + 1) * hd], MASKED)
                 S[d, at, c * hd : (c + 1) * hd] = val
                 best = val if best is None else jnp.maximum(best, val)
@@ -206,28 +215,31 @@
         out = (O2[at, :] * inv).astype(BF)
         att2[at, :] = out
         t0, h = (r % per_head) * tile, r // per_head
-        att_o[t0 : t0 + tile, h * hd : (h + 1) * hd] = out
-
-    def project(f):
-        term = dot(sc[f], w[:, f * fs : (f + 1) * fs], NT)
+        att[t0 : t0 + tile, h * hd : (h + 1) * hd] = out
+        for p in range(t0 // part, (t0 + tile) // part):
+            att_o[chunk_of(p), h * hd : (h + 1) * hd] = out[p * part - t0 : (p + 1) * part - t0]
+
+    def project(f, g=None):
+        at = pl.ds(0, rows) if g is None else pl.ds(g * tile, tile)
+        term = dot(sc[f, at, :], w[:, f * fs : (f + 1) * fs], NT)
         if f == 0:
-            dA[...] = term
+            dA[at, :] = term
         else:
-            dA[...] += term
+            dA[at, :] += term
 
     def pair_copy(f):
         return remote(psend.at[f], precv.at[f], pp_sem.at[0, f], pp_sem.at[1, f], sib_dev)
 
     def weight_rows(f, j, which):
-        width = att_o.shape[1]
+        width = att.shape[1]
         at = pl.ds(pl.multiple_of((2 * (j % 2) + which) * own_rows, own_rows), own_rows)
         return S[BACK - f, at, (j // 2) * width : (j // 2 + 1) * width]
 
     def weight_grad(f):
-        width = att_o.shape[1]
+        width = att.shape[1]
         cut = fs // 2
         for i in range(fs // hd):
-            term = dot(sc[f, :, i * hd : (i + 1) * hd], att_o[...], TN)
+            term = dot(sc[f, :, i * hd : (i + 1) * hd], att[...], TN)
             for side in (0, 1):
                 first, last = max(i * hd, side * cut), min((i + 1) * hd, (side + 1) * cut)
                 if first < last:
@@ -279,9 +291,21 @@
             xsend[f] = total.astype(BF)
             col_copy(f).start()
 
-    def backward(d, out, first=False):
-        for r in range(tiles):
-            at = pl.ds(r * tile, tile)
+    def ready(g):
+        for h in range(2):
+            at = pl.ds(h * rows + g * tile, tile)
+            rounded = dA[pl.ds(g * tile, tile), h * hd : (h + 1) * hd].astype(BF).astype(F32)
+            scaled = (rounded * rl[at, :]).astype(BF)
+            dAs[at, :] = scaled
+            wide = scaled.astype(F32)
+            dAsT[:, at] = wide.T.astype(BF)
+            d = jnp.sum(wide * att2[at, :].astype(F32), axis=1, keepdims=True)
+            delta[at, :] = jnp.broadcast_to(d, (tile, hd))
+
+    def backward(d, g, out, first=False):
+        dk_part, dv_part = 0.0, 0.0
+        for h in range(2):
+            at = pl.ds(h * rows + g * tile, tile)
             raw = dot(dAs[at, :], kv[d, :, hd:], NT)
             low = delta[at, :]
             for c in range(rows // hd):
@@ -292,8 +316,15 @@
                 dq[at, :] = term
             else:
                 dq[at, :] += term
-        out[:hd, :] = dot(qT[...], dS[...], NN).astype(out.dtype)
-        out[hd:, :] = dot(dAsT[...], Pb[d], NN).astype(out.dtype)
+            dk_part += dot(qT[:, at], dS[at, :], NN)
+            dv_part += dot(dAsT[:, at], Pb[d, at, :], NN)
+        if g:
+            dk_part, dv_part = ebuf[d, :hd, :] + dk_part, ebuf[d, hd:, :] + dv_part
+        out[:hd, :] = dk_part.astype(out.dtype)
+        out[hd:, :] = dv_part.astype(out.dtype)
+
+    def early(d, first=False):
+        backward(d, 0, ebuf.at[d], first)
 
     def sib_copy(i):
         return remote(ssend.at[i], srecv.at[i], ss_sem.at[0, i], ss_sem.at[1, i], sib_dev)
@@ -309,7 +340,7 @@
         return remote(half(lsend, h), half(lrecv, h), ll_sem.at[0, h], ll_sem.at[1, h], col_dev(-1))
 
     def odd(i, first=False):
-        backward(2 * i - 1, ssend.at[i], first)
+        backward(2 * i - 1, 1, ssend.at[i], first)
         sib_copy(i).start()
 
     def send_back(i):
@@ -317,7 +348,7 @@
         sib_copy(j).wait_recv()
         for h in (0, 1):
             hs_ = pl.ds(h * hd, hd)
-            rsend[i, hs_, :] = (ebuf[i, hs_, :] + srecv[j, hs_, :].astype(F32)).astype(BF)
+            rsend[i, hs_, :] = (ebuf[2 * i, hs_, :] + srecv[j, hs_, :].astype(F32)).astype(BF)
             back_copy(i, h).start()
 
     def relay_in():
@@ -376,49 +407,51 @@
     weigh(3, True)
     weight_grad(0)
     event(3, 2)
-
+    project(2, 0)
     weight_grad(1)
     row_send(0)
     event(2, 3)
+    project(3, 0)
+    ready(0)
+    early(7, True)
     row_send(1)
+    early(5)
+    early(6)
     arrived(3, 2)
-    project(2)
+    project(2, 1)
+    event(3, 3)
     weight_grad(2)
+    early(3)
+    early(4)
+    row_send(2)
+    early(1)
     col_send(0)
-    event(3, 3)
-    row_send(2)
-    col_send(1)
+    early(8)
+    early(2)
+    early(0)
     arrived(3, 3)
-    project(3)
-
-    for h in range(2):
-        hr = slice(h * rows, (h + 1) * rows)
-        rounded = dA[:, h * hd : (h + 1) * hd].astype(BF).astype(F32)
-        scaled = (rounded * rl[hr, :]).astype(BF)
-        dAs[hr, :] = scaled
-        wide = scaled.astype(F32)
-        dAsT[:, hr] = wide.T.astype(BF)
-        d = jnp.sum(wide * att2[hr, :].astype(F32), axis=1, keepdims=True)
-        delta[hr, :] = jnp.broadcast_to(d, (rows, hd))
-
+    project(3, 1)
+    ready(1)
     odd(4, True)
+    weight_grad(3)
     odd(3)
-    backward(6, ebuf.at[3])
+    backward(6, 1, ebuf.at[6])
     send_back(3)
-    weight_grad(3)
+    row_send(3)
     odd(2)
-    backward(4, ebuf.at[2])
+    backward(4, 1, ebuf.at[4])
     send_back(2)
     odd(1)
+    backward(2, 1, ebuf.at[2])
+    send_back(1)
+    backward(8, 1, ebuf.at[8])
+    backward(0, 1, ebuf.at[0])
+    col_send(1)
     col_send(2)
-    row_send(3)
-    backward(8, ebuf.at[4])
-    backward(2, ebuf.at[1])
-    send_back(1)
-    backward(0, ebuf.at[0])
-    for h in range(2):
-        hr = slice(h * rows, (h + 1) * rows)
-        dq_o[:, h * hd : (h + 1) * hd] = (dq[hr, :] * SCALE).astype(BF)
+    for p in range(RING):
+        for h in range(2):
+            grad = dq[pl.ds(h * rows + p * part, part), :] * SCALE
+            dq_o[chunk_of(p), h * hd : (h + 1) * hd] = grad.astype(BF)
 
     @pl.when(core == 1)
     def _():
@@ -426,7 +459,7 @@
 
     for h in (0, 1):
         hr = pl.ds(h * hd, hd)
-        total = ebuf[4, hr, :] + jnp.where(core == 1, srecv[4, hr, :].astype(F32), 0.0)
+        total = ebuf[8, hr, :] + jnp.where(core == 1, srecv[4, hr, :].astype(F32), 0.0)
         for i in (3, 2):
             back_copy(i, h).wait_recv()
             total = total + jnp.where(y + i >= SIDE, rrecv[i, hr, :].astype(F32), 0.0)
@@ -460,7 +493,7 @@
     for f in range(slices):
         for way in (0, 1):
             for kind in range(4):
-                ring_copy(way, kind, f, kind).wait_send()
+                ring_copy(way, kind, f).wait_send()
         pair_copy(f).wait_send()
         for i in (1, 2, 3):
             row_copy(f, i).wait_send()
@@ -511,11 +544,13 @@
         in_specs=[smem, smem, vmem, vmem, vmem, anywhere, vmem],
         out_specs=[vmem] * 5,
         scratch_shapes=[
+            V((rows, width), BF),
             V((slices, rows, fs), BF),
             V((width, depth), BF),
             V((BACK + 1, rows, 2 * hd), BF),
             V((q_rows, hd), BF),
             V((hd, q_rows), BF),
+            V((rows, hd), jnp.int32),
             V((rows, hd), jnp.int32),
             V((BACK + 1, q_rows, rows), F32),
             V((BACK + 1, q_rows, rows), BF),

time: 96.2 us -> 96.3 us (level)
  no operation moved by 1% of the time
where the time goes in v3:
time: 96.3 us; the launch traced here: 95.4 us
  Pallas kernels  94.8 us (98%)
    pallas_call x1, Pallas kernels, per_device(): pl.pallas_call(kernel, out_shape=[jax.ShapeDtypeStruct((rows, width), BF)...  92.6 us
    pallas_call x1, Pallas kernels, per_device(): pl.pallas_call(finish, out_shape=[jax.ShapeDtypeStruct((rows, heads, hd),...  2.12 us

profile of v3, /device:TPU:6, one launch (start us, length us, event | category | flops | bytes accessed | tf_op | source)
XLA Modules:
  0.0 95.4 jit_solution(16298463386339831159)
XLA Ops:
  0.6 92.6 %rollout_attention.1 = (bf16[512,256]{1,0:T(8,128)(2,1)}, bf16[512,256]{1,0:T(8,128)(2,1)}, bf16[512,128]{1,0:T(8,128)(2,1)}, bf16[512,128]{1,0:T(8,128)(2,1)}, f32[144,256]{1,0:T(8,128)}) custom-call(s32[8]{0:T(128)} %lens.1, f32[8]{0:T(128)} %adv.1, bf16[512,2,128]{2,1,0:T(2,128)(2,1)} %q_ref.1, bf16[512,128]{1,0:T(8,128)(2,1)} %bitcast.4, ...), custom_call_target="tpu_custom_call" | custom-call | flops 8999999488 | bytes 5000000 | tf_op jit(solution)/shard_map/rollout_attention/pallas_call | solution.py:535
  93.3 2.1 %lay_out_results.1 = (bf16[512,2,128]{2,1,0:T(2,128)(2,1)}, bf16[512,2,128]{2,1,0:T(2,128)(2,1)}, bf16[512,128]{1,0:T(8,128)(2,1)}, bf16[512,128]{1,0:T(8,128)(2,1)}, f32[144,256]{1,0:T(8,128)}) custom-call(bf16[512,256]{1,0:T(8,128)(2,1)} %get-tuple-element.15.refs_0_, bf16[512,256]{1,0:T(8,128)(2,1)} %get-tuple-element.16.refs_1_, ...), custom_call_target="tpu_custom_call" | custom-call | tf_op jit(solution)/shard_map/lay_out_results/pallas_call | solution.py:601

commit v4 on v2

--- a/solution.py
+++ b/solution.py
@@ -28,14 +28,15 @@
 
 
 def kernel(
-    lens, adv, q_ref, k_ref, v_ref, w_hbm, cot_ref,
-    att_o, dq_o, dk_o, dv_o, dwo_o,
+    lens, adv, q_hbm, k_hbm, v_hbm, w_hbm, cot_hbm,
+    att_hbm, dq_hbm, dk_hbm, dv_hbm, dwo_hbm,
+    q_ref, cot_ref, att_o, dq_o, dk_o, dv_o, dwo_o,
     sc, w, kv, q2, qT, lo, S, Pb, mx, rl, O2, att2,
     dA, dAs, dAsT, delta, dq, dS,
     psend, precv, ysend, yrecv, yown, xsend, xrecv, xown,
     ssend, srecv, rsend, rrecv, lsend, lrecv,
     gs_sem, gr_sem, w_sem, hx_sem, hy_sem, hs_sem,
-    pp_sem, yy_sem, xs_sem, xr_sem, ss_sem, rr_sem, ll_sem,
+    pp_sem, yy_sem, xs_sem, xr_sem, ss_sem, rr_sem, ll_sem, in_sem, out_sem,
 ):
     s = lax.axis_index("seq")
     z = lax.axis_index("tp")
@@ -44,10 +45,10 @@
     y = lax.rem(chip, SIDE)
     x = chip // SIDE
     rows, fs = sc.shape[1], sc.shape[2]
-    ebuf = S.at[:, : 2 * k_ref.shape[1], :]
+    ebuf = S.at[:, : 2 * k_hbm.shape[1], :]
     slices = sc.shape[0]
     part = rows // RING
-    hd = k_ref.shape[1]
+    hd = k_hbm.shape[1]
     own_rows = dwo_o.shape[0]
 
     def row_dev(i):
@@ -73,7 +74,18 @@
     for dev in [sib_dev, ring_dev(1), ring_dev(-1), next_dev] + around:
         pl.semaphore_signal(barrier, inc=1, device_id=dev, device_id_type=MESH)
     w_copy = pltpu.make_async_copy(w_hbm, w, w_sem)
-    w_copy.start()
+    cot_in = pltpu.make_async_copy(cot_hbm, cot_ref, in_sem.at[0])
+    k_in = pltpu.make_async_copy(k_hbm, kv.at[0, :, pl.ds(0, hd)], in_sem.at[1])
+    v_in = pltpu.make_async_copy(v_hbm, kv.at[0, :, pl.ds(hd, hd)], in_sem.at[2])
+    q_in = pltpu.make_async_copy(q_hbm, q_ref, in_sem.at[3])
+    for copy in (cot_in, k_in, v_in, q_in, w_copy):
+        copy.start()
+    leaving = [
+        pltpu.make_async_copy(ref, out, out_sem.at[i])
+        for i, (ref, out) in enumerate(
+            ((att_o, att_hbm), (dq_o, dq_hbm), (dk_o, dk_hbm), (dv_o, dv_hbm), (dwo_o, dwo_hbm))
+        )
+    ]
 
     place = s * rows + z * part + lax.broadcasted_iota(jnp.int32, (part, hd), 0)
     factor = jnp.full((part, hd), adv[0], F32)
@@ -83,11 +95,10 @@
         factor = jnp.where(place >= cum, adv[r + 1], factor)
     wide = jnp.concatenate([factor] * (fs // hd), axis=1)
     my_rows = pl.ds(pl.multiple_of(z * part, part), part)
+    cot_in.wait()
     for f in range(slices):
         piece = cot_ref[:, f * fs : (f + 1) * fs].astype(F32)
         sc[f, my_rows, :] = (wide * piece).astype(BF)
-    kv[0, :, :hd] = k_ref[...]
-    kv[0, :, hd:] = v_ref[...]
 
     pl.semaphore_wait(barrier, 10)
 
@@ -116,6 +127,9 @@
     event(0, 0)
     event(0, 1)
 
+    k_in.wait()
+    v_in.wait()
+
     def hx():
         return remote(kv.at[0], kv.at[8], hx_sem.at[0], hx_sem.at[1], col_dev(1))
 
@@ -140,6 +154,7 @@
     def _():
         hs(0).start()
 
+    q_in.wait()
     q2[:rows, :] = q_ref[:, 0, :]
     q2[rows:, :] = q_ref[:, 1, :]
     qT[...] = q2[...].astype(F32).T.astype(BF)
@@ -374,6 +389,7 @@
     arrived(3, 1)
     project(1)
     weigh(3, True)
+    leaving[0].start()
     weight_grad(0)
     event(3, 2)
 
@@ -419,6 +435,7 @@
     for h in range(2):
         hr = slice(h * rows, (h + 1) * rows)
         dq_o[:, h * hd : (h + 1) * hd] = (dq[hr, :] * SCALE).astype(BF)
+    leaving[1].start()
 
     @pl.when(core == 1)
     def _():
@@ -438,6 +455,7 @@
         col_from(i).wait_recv()
         own = own + xrecv[i].astype(F32)
     dwo_o[...] = own
+    leaving[4].start()
 
     @pl.when(core == 0)
     def _():
@@ -454,8 +472,10 @@
         total = total + lrecv[hr, :].astype(F32)
         if h == 0:
             dk_o[...] = (total.T * SCALE).astype(BF)
+            leaving[2].start()
         else:
             dv_o[...] = total.T.astype(BF)
+            leaving[3].start()
 
     for f in range(slices):
         for way in (0, 1):
@@ -478,6 +498,8 @@
         sib_copy(j).wait_send()
     for h in (0, 1):
         relay(h).wait_send()
+    for copy in leaving:
+        copy.wait()
 
 
 def finish(*refs):
@@ -489,7 +511,7 @@
 def per_device(queries, keys, values, out_weight, cotangent, advantages, lengths):
     rows, heads, hd = queries.shape
     width = heads * hd
-    depth = cotangent.shape[1]
+    part, depth = cotangent.shape
     slices = SIDE
     fs = depth // slices
     own = depth // lax.axis_size("seq")
@@ -508,9 +530,16 @@
             jax.ShapeDtypeStruct((rows, hd), BF),
             jax.ShapeDtypeStruct((own, width), F32),
         ],
-        in_specs=[smem, smem, vmem, vmem, vmem, anywhere, vmem],
-        out_specs=[vmem] * 5,
+        in_specs=[smem, smem] + [anywhere] * 5,
+        out_specs=[anywhere] * 5,
         scratch_shapes=[
+            V((rows, heads, hd), BF),
+            V((part, depth), BF),
+            V((rows, width), BF),
+            V((rows, width), BF),
+            V((rows, hd), BF),
+            V((rows, hd), BF),
+            V((own, width), F32),
             V((slices, rows, fs), BF),
             V((width, depth), BF),
             V((BACK + 1, rows, 2 * hd), BF),
@@ -556,6 +585,8 @@
             dma((2, 5)),
             dma((2, 4, 2)),
             dma((2, 2)),
+            dma((4,)),
+            dma((5,)),
         ],
         compiler_params=pltpu.CompilerParams(
             collective_id=0, has_side_effects=True, vmem_limit_bytes=60 * 1024 * 1024

time: 96.2 us -> 95.3 us (level)
  no operation moved by 1% of the time
where the time goes in v4:
time: 95.3 us; the launch traced here: 95.2 us
  Pallas kernels  94.5 us (99%)
    pallas_call x1, Pallas kernels, per_device(): pl.pallas_call(kernel, out_shape=[jax.ShapeDtypeStruct((rows, width), BF)...  92.4 us
    pallas_call x1, Pallas kernels, per_device(): pl.pallas_call(finish, out_shape=[jax.ShapeDtypeStruct((rows, heads, hd),...  2.12 us

profile of v4, /device:TPU:6, one launch (start us, length us, event | category | flops | bytes accessed | tf_op | source)
XLA Modules:
  0.0 95.2 jit_solution(13170672275371671521)
XLA Ops:
  0.6 92.4 %rollout_attention.1 = (bf16[512,256]{1,0:T(8,128)(2,1)}, bf16[512,256]{1,0:T(8,128)(2,1)}, bf16[512,128]{1,0:T(8,128)(2,1)}, bf16[512,128]{1,0:T(8,128)(2,1)}, f32[144,256]{1,0:T(8,128)}) custom-call(s32[8]{0:T(128)} %lens.1, f32[8]{0:T(128)} %adv.1, bf16[512,2,128]{2,1,0:T(2,128)(2,1)} %q_hbm.1, bf16[512,128]{1,0:T(8,128)(2,1)} %bitcast.4, ...), custom_call_target="tpu_custom_call" | custom-call | flops 8999999488 | bytes 5000000 | tf_op jit(solution)/shard_map/rollout_attention/pallas_call | solution.py:524
  93.1 2.1 %lay_out_results.1 = (bf16[512,2,128]{2,1,0:T(2,128)(2,1)}, bf16[512,2,128]{2,1,0:T(2,128)(2,1)}, bf16[512,128]{1,0:T(8,128)(2,1)}, bf16[512,128]{1,0:T(8,128)(2,1)}, f32[144,256]{1,0:T(8,128)}) custom-call(bf16[512,256]{1,0:T(8,128)(2,1)} %get-tuple-element.15.refs_0_, bf16[512,256]{1,0:T(8,128)(2,1)} %get-tuple-element.16.refs_1_, ...), custom_call_target="tpu_custom_call" | custom-call | tf_op jit(solution)/shard_map/lay_out_results/pallas_call | solution.py:597

commit v5 on v3

--- a/solution.py
+++ b/solution.py
@@ -432,12 +432,12 @@
     arrived(3, 3)
     project(3, 1)
     ready(1)
+    weight_grad(3)
     odd(4, True)
-    weight_grad(3)
+    row_send(3)
     odd(3)
     backward(6, 1, ebuf.at[6])
     send_back(3)
-    row_send(3)
     odd(2)
     backward(4, 1, ebuf.at[4])
     send_back(2)
@@ -445,9 +445,10 @@
     backward(2, 1, ebuf.at[2])
     send_back(1)
     backward(8, 1, ebuf.at[8])
+    col_send(1)
     backward(0, 1, ebuf.at[0])
-    col_send(1)
     col_send(2)
+    col_send(3)
     for p in range(RING):
         for h in range(2):
             grad = dq[pl.ds(h * rows + p * part, part), :] * SCALE
@@ -465,7 +466,6 @@
             total = total + jnp.where(y + i >= SIDE, rrecv[i, hr, :].astype(F32), 0.0)
         lsend[hr, :] = total.astype(BF)
         relay(h).start()
-    col_send(3)
     own = xown[...]
     for i in (1, 2, 3):
         col_from(i).wait_recv()

time: 96.3 us -> 93.3 us (0.969)
  Pallas kernels: 94.8 us -> 91.7 us
    pallas_call x1, Pallas kernels: 92.6 us -> 89.6 us  [per_device(): pl.pallas_call(kernel, out_shape=[jax.ShapeDtypeStruct((rows, width), BF)...]
where the time goes in v5:
time: 93.3 us; the launch traced here: 92.3 us
  Pallas kernels  91.7 us (98%)
    pallas_call x1, Pallas kernels, per_device(): pl.pallas_call(kernel, out_shape=[jax.ShapeDtypeStruct((rows, width), BF)...  89.6 us
    pallas_call x1, Pallas kernels, per_device(): pl.pallas_call(finish, out_shape=[jax.ShapeDtypeStruct((rows, heads, hd),...  2.12 us

profile of v5, /device:TPU:6, one launch (start us, length us, event | category | flops | bytes accessed | tf_op | source)
XLA Modules:
  0.0 92.3 jit_solution(14718649050918860381)
XLA Ops:
  0.6 89.6 %rollout_attention.1 = (bf16[512,256]{1,0:T(8,128)(2,1)}, bf16[512,256]{1,0:T(8,128)(2,1)}, bf16[512,128]{1,0:T(8,128)(2,1)}, bf16[512,128]{1,0:T(8,128)(2,1)}, f32[144,256]{1,0:T(8,128)}) custom-call(s32[8]{0:T(128)} %lens.1, f32[8]{0:T(128)} %adv.1, bf16[512,2,128]{2,1,0:T(2,128)(2,1)} %q_ref.1, bf16[512,128]{1,0:T(8,128)(2,1)} %bitcast.4, ...), custom_call_target="tpu_custom_call" | custom-call | flops 8999999488 | bytes 5000000 | tf_op jit(solution)/shard_map/rollout_attention/pallas_call | solution.py:535
  90.2 2.1 %lay_out_results.1 = (bf16[512,2,128]{2,1,0:T(2,128)(2,1)}, bf16[512,2,128]{2,1,0:T(2,128)(2,1)}, bf16[512,128]{1,0:T(8,128)(2,1)}, bf16[512,128]{1,0:T(8,128)(2,1)}, f32[144,256]{1,0:T(8,128)}) custom-call(bf16[512,256]{1,0:T(8,128)(2,1)} %get-tuple-element.15.refs_0_, bf16[512,256]{1,0:T(8,128)(2,1)} %get-tuple-element.16.refs_1_, ...), custom_call_target="tpu_custom_call" | custom-call | tf_op jit(solution)/shard_map/lay_out_results/pallas_call | solution.py:601
